TPU v7x, 128 devices: a whole 4x4x4 slice. The times are simulated.
128 devices in a mesh: tensor: 8 (over y, x_lo), context: 16 (over x_hi, z, core).
Axes of the slice: x: 4 (x_hi: 2, x_lo: 2; x = x_hi * 2 + x_lo), y: 4, z: 4, core: 2. Of those that a mesh axis runs over, the one named last changes fastest.
Arguments:
- teacher_in: bfloat16 [16384, 4096], P('context', 'tensor'), may hold values from -6 to 6
- teacher_resid: bfloat16 [16384, 8192], P('context', 'tensor'), may hold values from -17 to 17
- teacher_wo: bfloat16 [4096, 8192], P('tensor'), may hold values from -0.09375 to 0.09375
- teacher_gain: float32 [8192], replicated, may hold values from 0.5 to 1.5
- input_history: float32 [16], replicated, may hold values from 1.5 to 3.5
- weight_history: float32 [16], replicated, as said below
- student_hidden: bfloat16 [16384, 4096], P(('context', 'tensor')), may hold values from -24 to 24
- student_gain: float32 [4096], replicated, may hold values from 0.5 to 1.5
- projection: bfloat16 [4096, 8192], P('context', 'tensor'), may hold values from -0.09375 to 0.09375
Outputs:
- proj_grad: float32 [4096, 8192], P('context', 'tensor')
- distill_loss: float32 [], replicated
- input_history_new: float32 [16], replicated
- weight_history_new: float32 [16], replicated
Inputs may be any that keep to these rules, and one draw needn't show every extreme that they name: `weight_history`: entries lie between 1.6 and 3.2 times 4096 ** -0.5.
All inputs are finite; a program needn't handle non-finite values.
Results may differ from a plain program's by a relative error of at most 0.018.
Values may be sent and summed in bfloat16 or wider, within the bound.
A program may use at most 192 MiB of HBM per device.

v0:
```python
import math

import jax
import jax.numpy as jnp
from jax import lax
from jax.sharding import PartitionSpec as P


def normalize(hidden_rows, gain_row):
    return (
        hidden_rows
        * lax.rsqrt(jnp.mean(hidden_rows * hidden_rows, axis=-1, keepdims=True) + 1e-05)
        * gain_row
    )


def local(
    teacher_in,
    teacher_resid,
    teacher_wo,
    teacher_gain,
    input_history,
    weight_history,
    student_hidden,
    student_gain,
    projection,
):
    local_input = jnp.max(jnp.abs(teacher_in.astype(jnp.float32)))
    local_weight = jnp.max(jnp.abs(teacher_wo.astype(jnp.float32)))
    input_amax = lax.pmax(local_input, ("tensor", "context"))
    weight_amax = lax.pmax(local_weight, "tensor")
    input_history_new = jnp.concatenate([input_amax.reshape(1), input_history[:-1]])
    weight_history_new = jnp.concatenate([weight_amax.reshape(1), weight_history[:-1]])
    input_limit = jnp.max(input_history)
    weight_limit = jnp.max(weight_history)
    input_sat = jnp.clip(teacher_in.astype(jnp.float32), -input_limit, input_limit).astype(
        jnp.bfloat16
    )
    weight_sat = jnp.clip(teacher_wo.astype(jnp.float32), -weight_limit, weight_limit).astype(
        jnp.bfloat16
    )
    group_len = input_sat.shape[0]
    tensor_count = lax.axis_size("tensor")
    feature_len = teacher_resid.shape[1]
    partial_value = jnp.dot(input_sat, weight_sat, preferred_element_type=jnp.float32)
    projected = lax.psum_scatter(
        partial_value.astype(jnp.bfloat16), "tensor", scatter_dimension=1, tiled=True
    ).astype(jnp.float32)
    hidden = teacher_resid.astype(jnp.float32) + projected
    squares = lax.psum(jnp.sum(hidden * hidden, axis=1), "tensor")
    full_width = feature_len * tensor_count
    gain_row = lax.dynamic_slice_in_dim(
        teacher_gain, lax.axis_index("tensor") * feature_len, feature_len, 0
    )
    target = hidden * lax.rsqrt(squares / full_width + 1e-05)[:, None] * gain_row
    student_norm = normalize(student_hidden.astype(jnp.float32), student_gain).astype(jnp.bfloat16)
    group_rows = lax.all_gather(student_norm, "tensor", axis=0, tiled=True)
    columns = group_rows
    mapped = jnp.dot(
        columns,
        lax.all_gather(projection, "context", axis=0, tiled=True),
        preferred_element_type=jnp.float32,
    )
    error = mapped - target
    error_sum = lax.psum(jnp.sum(error * error), ("tensor", "context"))
    context_count = lax.axis_size("context")
    length_all = group_len * context_count
    distill_loss = 0.5 * error_sum / (length_all * feature_len * tensor_count)
    error_low = error.astype(jnp.bfloat16)
    columns = group_rows
    summed = lax.psum_scatter(
        lax.dot_general(
            columns, error_low, (((0,), (0,)), ((), ())), preferred_element_type=jnp.float32
        ).astype(jnp.bfloat16),
        "context",
        scatter_dimension=0,
        tiled=True,
    ).astype(jnp.float32)
    proj_grad = summed * (1.0 / math.sqrt(length_all))
    return (proj_grad, distill_loss, input_history_new, weight_history_new)


def solution(mesh):
    placed = (
        P("context", "tensor"),
        P("context", "tensor"),
        P("tensor", None),
        P(),
        P(),
        P(),
        P(("context", "tensor"), None),
        P(),
        P("context", "tensor"),
    )
    return jax.shard_map(
        local,
        mesh=mesh,
        in_specs=placed,
        out_specs=(P("context", "tensor"), P(), P(), P()),
        check_vma=False,
    )
```

profile of v0, /device:TPU:0, one launch (start us, length us, event | category | flops | bytes accessed | tf_op | source)
XLA Modules:
  0.0 804.8 jit_solution(16291843978972727912)
XLA Ops:
  7.2 1.3 reduce_max.36
  9.1 1.3 reduce_max.37
  11.0 16.1 %convolution_convert_fusion = bf16[1024,8192]{1,0:T(8,128)(2,1)} fusion(bf16[512,8192]{1,0:T(8,128)(2,1)} %param.11, bf16[]{:T(256)S(6)} %neg.7, f32[]{:T(128)} %reduce_max.37, bf16[1024,512]{1,0:T(8,128)(2,1)} %param.9, bf16[]{:T(256)S(6)} %neg.6, f32[]{:T(128)} %reduce_max.36), kind=kOutput, calls=%fused_computation.5 | convolution fusion | flops 8626634752 | bytes 26214412 | tf_op jit(solution)/shard_map/dot_general | solution.py:45
  27.2 0.0 all-gather.3.cloned.1.call-start
  27.3 1.1 copy-done
  28.4 0.3 fusion.6
  28.7 1.3 fusion.8
  30.1 0.7 all-gather.5.cloned.1.call-update
  30.9 325.4 %reduce-scatter.3.cloned.1.call-done = bf16[1024,1024]{1,0:T(8,128)(2,1)} async-done(((bf16[1024,8192]{1,0:T(8,128)(2,1)}), bf16[1024,1024]{1,0:T(8,128)(2,1)}) %reduce-scatter.3.cloned.1.call-update) | async-done | bytes 2097168 | tf_op jit(solution)/shard_map/reduce_scatter | solution.py:46
  356.3 2.3 multiply_reduce_fusion.1
  358.6 18.8 %psum.14 = f32[1024]{0:T(1024)S(1)} all-reduce(f32[1024]{0:T(1024)S(1)} %multiply_reduce_fusion.1), channel_id=1, replica_groups=mesh['tensor'=8,'context'=16] {'tensor'}, use_global_device_ids=true, to_apply=%region_5.0 | all-reduce | flops 1024 | bytes 8192 | tf_op jit(solution)/shard_map/psum | solution.py:50
  377.4 150.6 %all-gather.3.cloned.1.call-done = bf16[1024,4096]{1,0:T(8,128)(2,1)} async-done(((bf16[128,4096]{1,0:T(8,128)(2,1)}), bf16[1024,4096]{1,0:T(8,128)(2,1)}) %all-gather.3.cloned.1.call-update) | async-done | bytes 8388624 | tf_op jit(solution)/shard_map/all_gather | solution.py:57
  528.0 76.6 %all-gather.5.cloned.1.call-done = bf16[4096,1024]{1,0:T(8,128)(2,1)} async-done(((bf16[256,1024]{1,0:T(8,128)(2,1)}), bf16[4096,1024]{1,0:T(8,128)(2,1)}) %all-gather.5.cloned.1.call-update) | async-done | bytes 8388624 | tf_op jit(solution)/shard_map/all_gather | solution.py:61
  604.6 15.6 %multiply_reduce_fusion = (f32[]{:T(128)}, bf16[1024,1024]{1,0:T(8,128)(2,1)S(1)}) fusion(f32[1024]{0:T(1024)S(1)} %dynamic-slice-done, f32[1024]{0:T(1024)S(1)} %add_rsqrt_fusion, bf16[1024,1024]{1,0:T(8,128)(2,1)} %reduce-scatter.3.cloned.1.call-done, bf16[1024,1024]{1,0:T(8,128)(2,1)S(1)} %copy-done.1, ...), kind=kOutput, calls=%fused_computation.9 | convolution fusion | flops 8599371776 | bytes 23076868 | tf_op jit(solution)/shard_map/dot_general | solution.py:59
  620.3 11.3 %convolution_convert_fusion.1 = bf16[4096,1024]{1,0:T(8,128)(2,1)} fusion(bf16[1024,4096]{1,0:T(8,128)(2,1)S(1)} %copy-done.4, bf16[1024,1024]{1,0:T(8,128)(2,1)S(1)} %get-tuple-element.5), kind=kOutput, calls=%fused_computation.8 | convolution fusion | flops 8594128896 | bytes 18874368 | tf_op jit(solution)/shard_map/dot_general | solution.py:72
  631.6 1.2 copy-done.2
  632.8 0.7 fusion.11
  633.5 71.9 %pmax.14 = f32[1]{0:T(128)} all-reduce(f32[1]{0:T(128)} %bitcast), channel_id=1, replica_groups=mesh['tensor'=8,'context'=16] {'tensor','context'}, use_global_device_ids=true, to_apply=%region_10.11 | all-reduce | flops 1 | bytes 8 | tf_op jit(solution)/shard_map/pmax | solution.py:30
  705.4 5.2 fusion.2
  710.6 18.3 %pmax.15 = f32[1]{0:T(128)} all-reduce(f32[1]{0:T(128)} %bitcast.1), channel_id=1, replica_groups=mesh['tensor'=8,'context'=16] {'tensor'}, use_global_device_ids=true, to_apply=%region_12.13 | all-reduce | flops 1 | bytes 8 | tf_op jit(solution)/shard_map/pmax | solution.py:31
  728.9 1.2 pad_maximum_fusion
  730.1 1.2 pad_maximum_fusion.1
  731.3 62.9 %psum.15 = f32[]{:T(128)} all-reduce(f32[]{:T(128)} %get-tuple-element.4), channel_id=1, replica_groups=mesh['tensor'=8,'context'=16] {'tensor','context'}, use_global_device_ids=true, to_apply=%region_8.9 | all-reduce | flops 1 | bytes 8 | tf_op jit(solution)/shard_map/psum | solution.py:65
  795.0 2.1 convert_multiply_fusion.2
  (23 shorter events, 0.2 us)
Async XLA Ops:
  7.2 349.1 %reduce-scatter.3.cloned.1.call-start = ((), (), s32[]{:S(2)}) async-start(), calls=%async_computation.4 | async-start | bytes 18874368 | tf_op jit(solution)/shard_map/reduce_scatter | solution.py:46
  27.2 1.2 copy-start
  27.2 1.5 copy-start.3
  27.2 329.0 %copy-start.1 = (bf16[1024,1024]{1,0:T(8,128)(2,1)S(1)}, bf16[1024,1024]{1,0:T(8,128)(2,1)}, u32[]{:S(2)}) copy-start(bf16[1024,1024]{1,0:T(8,128)(2,1)} %param.10) | copy-start | bytes 6291460
  27.2 500.8 %all-gather.3.cloned.1.call-start = ((), (), s32[]{:S(2)}) async-start(), calls=%async_computation.2 | async-start | bytes 9437184 | tf_op jit(solution)/shard_map/all_gather | solution.py:57
  30.0 574.6 %all-gather.5.cloned.1.call-start = ((), (), s32[]{:S(2)}) async-start(), calls=%async_computation.3 | async-start | bytes 8912896 | tf_op jit(solution)/shard_map/all_gather | solution.py:61
  30.8 764.2 %reduce-scatter.5.cloned.1.call-start = ((), (), s32[]{:S(2)}) async-start(), calls=%async_computation.5 | async-start | bytes 8912896 | tf_op jit(solution)/shard_map/reduce_scatter | solution.py:71
  30.8 573.8 %dynamic-slice-start = ((f32[8192]{0:T(1024)}, s32[]{:T(128)}), f32[1024]{0:T(1024)S(1)}, s32[]{:S(2)}) async-start(f32[8192]{0:T(1024)} %param.12, s32[]{:T(128)} %select_n.3), calls=%async_computation.6 | async-start | bytes 8704 | tf_op jit(solution)/shard_map/dynamic_slice | solution.py:52
  604.6 15.6 %copy-start.4 = (bf16[1024,4096]{1,0:T(8,128)(2,1)S(1)}, bf16[1024,4096]{1,0:T(8,128)(2,1)}, u32[]{:S(2)}) copy-start(bf16[1024,4096]{1,0:T(8,128)(2,1)} %all-gather.3.cloned.1.call-done) | copy-start | bytes 25165828
  631.6 1.2 copy-start.2
  705.4 23.5 %copy-start.5 = (f32[16]{0:T(128)S(1)}, f32[16]{0:T(128)}, u32[]{:S(2)}) copy-start(f32[16]{0:T(128)} %param.13) | copy-start | bytes 196
  705.4 24.7 %copy-start.6 = (f32[16]{0:T(128)S(1)}, f32[16]{0:T(128)}, u32[]{:S(2)}) copy-start(f32[16]{0:T(128)} %param.14) | copy-start | bytes 196
Sparse Core Ops, SparseCore 0:
  27.3 328.8 reduce-scatter.2
  358.5 169.4 all-gather.2
  530.5 74.1 all-gather.4
  631.7 101.1 reduce-scatter.4
where the time goes:
time: 806 us; the launch traced here: 805 us
  waiting for transfers between devices  553 us (69%)
  blocking collectives  172 us (21%)
  matrix products  43.1 us (5%)
  other arithmetic  16.9 us (2%)
  between operations  16.9 us (2%)
    reduce_scatter x1, waiting for transfers between devices, local(): lax.psum_scatter(partial_value.astype(jnp.bfloat16), 'tensor', scatter_di...  325 us
    all_gather x1, waiting for transfers between devices, local(): group_rows = lax.all_gather(student_norm, 'tensor', axis=0, tiled=True)  151 us
    all_gather x1, waiting for transfers between devices, local(): lax.all_gather(projection, 'context', axis=0, tiled=True)  76.6 us
    pmax x1, blocking collectives, local(): input_amax = lax.pmax(local_input, ('tensor', 'context'))  71.9 us
    psum x1, blocking collectives, local(): error_sum = lax.psum(jnp.sum(error * error), ('tensor', 'context'))  62.9 us
    psum x1, blocking collectives, local(): squares = lax.psum(jnp.sum(hidden * hidden, axis=1), 'tensor')  18.8 us
    pmax x1, blocking collectives, local(): weight_amax = lax.pmax(local_weight, 'tensor')  18.3 us
    dot_general x1, matrix products, local(): jnp.dot(input_sat, weight_sat, preferred_element_type=jnp.float32)  16.1 us
  transfers between devices with their start and end apart: 4, of which 3 were waited for; matrix products, arithmetic and copies ran while one was open for 2% of the time, Pallas kernels for 0%

commit v1 on v0

v1 whole, which is shorter than its diff:
```python
import functools
import math

import jax
import jax.numpy as jnp
from jax import lax
from jax.experimental import pallas as pl
from jax.experimental.pallas import tpu as pltpu
from jax.sharding import PartitionSpec as P

MESH = pl.DeviceIdType.MESH
F32, BF16 = jnp.float32, jnp.bfloat16
EPS = 1e-05
COPIES = 100
XROWS = 80


def lanes(tile):
    rows, width = tile.shape
    return [
        tile[r : r + 8, c : c + 128]
        for r in range(0, rows, 8)
        for c in range(0, width, 128)
    ]


def fold(op, tile):
    parts = lanes(tile)
    while len(parts) > 1:
        parts = [op(a, b) for a, b in zip(parts[::2], parts[1::2])] + (
            [parts[-1]] if len(parts) % 2 else []
        )
    return parts[0]


def kernel(
    tokens_all,
    hist_in, hist_w, stu_gain, tea_gain, tin, resid, wo, stu, proj,
    grad, hist_in_new, hist_w_new, loss,
    T, W, S, PR, R, H, M, E, psend, precv, sraw, wraw, col, sq, scal, sib, rs, st,
    ssem, rsem, lsem,
):
    t, c = lax.axis_index("tensor"), lax.axis_index("context")
    y, xl = t // 2, t % 2
    xh, z, k = c // 8, (c // 2) % 4, c % 2

    def dev(dy=0, dxl=0, dxh=0, dz=0, dk=0):
        ny, nz = (y + dy) % 4, (z + dz) % 4
        nxl, nxh, nk = (xl + dxl) % 2, (xh + dxh) % 2, (k + dk) % 2
        return {"tensor": ny * 2 + nxl, "context": nxh * 8 + nz * 2 + nk}

    sends = []

    def send(src, dst, **to):
        i = len(sends)
        copy = pltpu.make_async_remote_copy(
            src_ref=src,
            dst_ref=dst,
            send_sem=ssem.at[i],
            recv_sem=rsem.at[i],
            device_id=dev(**to),
            device_id_type=MESH,
        )
        copy.start()
        sends.append(copy)
        return copy

    local = []

    def load(src, dst):
        copy = pltpu.make_async_copy(src, dst, lsem.at[len(local)])
        copy.start()
        local.append(copy)
        return copy

    TENSOR = [(dy, dx) for dy in range(4) for dx in range(2) if (dy, dx) != (0, 0)]
    CONTEXT = [(dx, dz) for dx in range(2) for dz in range(4) if (dx, dz) != (0, 0)]
    UP, DOWN = 1, 3

    j_own = 2 * z + k
    slab = pl.multiple_of(64 * j_own, 64)
    l_proj = load(proj, PR.at[pl.ds(pl.multiple_of(256 * c, 256), 256)])
    l_stu = load(stu, sraw)
    l_wraw = load(wo.at[pl.ds(slab, 64)], wraw)
    l_tin = load(tin, T.at[:, pl.ds(0, 512)])
    l_wown = load(wo.at[:, pl.ds(pl.multiple_of(2048 * y, 2048), 2048)], W.at[0])
    l_res = load(resid, R)

    barrier = pltpu.get_barrier_semaphore()
    for dy, dx in TENSOR:
        pl.semaphore_signal(barrier, 1, device_id=dev(dy=dy, dxl=dx), device_id_type=MESH)
    for dx, dz in CONTEXT:
        pl.semaphore_signal(barrier, 1, device_id=dev(dxh=dx, dz=dz), device_id_type=MESH)
    pl.semaphore_signal(barrier, 1, device_id=dev(dk=1), device_id_type=MESH)

    lim_in, lim_w = hist_in[0], hist_w[0]
    for i in range(1, 16):
        lim_in = jnp.maximum(lim_in, hist_in[i])
        lim_w = jnp.maximum(lim_w, hist_w[i])

    l_stu.wait()

    @pl.loop(0, 8)
    def _(i):
        rows = pl.ds(pl.multiple_of(16 * i, 16), 16)
        v = sraw[rows, :].astype(F32)
        mean = jnp.mean(v * v, axis=1, keepdims=True)
        S[0, rows, :] = (v * lax.rsqrt(mean + EPS) * stu_gain[...]).astype(BF16)

    pl.semaphore_wait(barrier, len(TENSOR) + len(CONTEXT) + 1)

    nx = XROWS
    ny = 128 - nx
    own_x, own_y = pl.ds(0, nx), pl.ds(nx, ny)
    far_x, far_y = pl.ds(128, nx), pl.ds(128 + nx, ny)
    sy_up = send(S.at[0, own_y], S.at[3, own_y], dy=UP)
    sy_dn = send(S.at[0, own_y], S.at[1, own_y], dy=DOWN)
    l_proj.wait()

    def pblock(dxh=0, dz=0):
        at = ((xh + dxh) % 2) * 8 + ((z + dz) % 4) * 2 + k
        return PR.at[pl.ds(pl.multiple_of(256 * at, 256), 256)]

    p_x = send(pblock(), pblock(), dxh=1)
    p_up = send(pblock(), pblock(), dz=UP)
    p_dn = send(pblock(), pblock(), dz=DOWN)
    p_sib = [send(pblock(), pblock(), dk=1)]
    sx = send(S.at[0, own_x], S.at[0, far_x], dxl=1)
    sxy = [send(S.at[0, own_y], S.at[0, far_y], dxl=1)]

    l_wraw.wait()

    def clip_w(i, amax):
        rows = pl.ds(pl.multiple_of(16 * i, 16), 16)
        for n in range(8):
            cols = pl.ds(1024 * n, 1024)
            v = wraw[rows, cols].astype(F32)
            amax = jnp.maximum(amax, fold(jnp.maximum, jnp.abs(v)))
            wraw[rows, cols] = jnp.clip(v, -lim_w, lim_w).astype(BF16)
        return amax

    amax_w = lax.fori_loop(0, 4, clip_w, jnp.zeros((8, 128), F32))

    def wcols(d):
        return pl.ds(pl.multiple_of(2048 * ((y + d) % 4), 2048), 2048)

    w_y = [
        send(wraw.at[:, wcols(d)], W.at[4 - d, pl.ds(slab, 64)], dy=d) for d in (1, 3, 2)
    ]

    l_tin.wait()

    def clip_t(i, amax):
        rows = pl.ds(pl.multiple_of(32 * i, 32), 32)
        v = T[rows, pl.ds(0, 512)].astype(F32)
        T[rows, pl.ds(0, 512)] = jnp.clip(v, -lim_in, lim_in).astype(BF16)
        return jnp.maximum(amax, fold(jnp.maximum, jnp.abs(v)))

    amax_in = lax.fori_loop(0, 32, clip_t, jnp.zeros((8, 128), F32))

    def tblock(r, rows=None):
        return T.at[pl.ds(0, 1024) if rows is None else rows, pl.ds(512 * r, 512)]

    t_up = send(tblock(0), tblock(3), dy=UP)
    t_dn = send(tblock(0), tblock(1), dy=DOWN)

    left, right = pl.ds(0, 2048), pl.ds(2048, 2048)
    sy_up.wait_recv()
    sy_up2 = send(S.at[3, own_y, left], S.at[2, own_y, left], dy=UP)
    sxy.append(send(S.at[3, own_y], S.at[3, far_y], dxl=1))
    sy_dn.wait_recv()
    sy_dn2 = send(S.at[1, own_y, right], S.at[2, own_y, right], dy=DOWN)
    sxy.append(send(S.at[1, own_y], S.at[1, far_y], dxl=1))

    p_x.wait_recv()
    q_up = send(pblock(1), pblock(1), dz=UP)
    q_dn = send(pblock(1), pblock(1), dz=DOWN)
    p_sib.append(send(pblock(1), pblock(1), dk=1))

    def wslab(dz=0, half=None):
        at = pl.multiple_of(64 * (2 * ((z + dz) % 4) + k), 64)
        if half is None:
            return W.at[pl.ds(1, 3), pl.ds(at, 64)]
        return W.at[pl.ds(1, 3), pl.ds(pl.multiple_of(at + 32 * half, 32), 32)]

    for copy in w_y:
        copy.wait_recv()
    w_up = send(wslab(), wslab(), dz=UP)
    w_dn = send(wslab(), wslab(), dz=DOWN)
    w_sib = [send(wslab(), wslab(), dk=1)]

    l_wown.wait()

    @pl.loop(0, 32)
    def _(i):
        rows = pl.ds(pl.multiple_of(16 * i, 16), 16)
        v = W[0, rows, :].astype(F32)
        W[0, rows, :] = jnp.clip(v, -lim_w, lim_w).astype(BF16)

    p_up.wait_recv()
    p_up2 = send(pblock(0, DOWN), pblock(0, DOWN), dz=UP)
    p_sib.append(send(pblock(0, DOWN), pblock(0, DOWN), dk=1))
    p_dn.wait_recv()
    p_sib.append(send(pblock(0, UP), pblock(0, UP), dk=1))
    sy_up2.wait_recv()
    sy_dn2.wait_recv()
    sxy.append(send(S.at[2, own_y], S.at[2, far_y], dxl=1))

    w_up.wait_recv()
    w_up2 = send(wslab(DOWN, 0), wslab(DOWN, 0), dz=UP)
    w_sib.append(send(wslab(DOWN), wslab(DOWN), dk=1))
    w_dn.wait_recv()
    w_dn2 = send(wslab(UP, 1), wslab(UP, 1), dz=DOWN)
    w_sib.append(send(wslab(UP), wslab(UP), dk=1))

    t_up.wait_recv()
    t_up2 = send(tblock(3, pl.ds(0, 512)), tblock(2, pl.ds(0, 512)), dy=UP)
    t_dn.wait_recv()
    t_dn2 = send(tblock(1, pl.ds(512, 512)), tblock(2, pl.ds(512, 512)), dy=DOWN)

    a_up = send(S.at[0, own_x], S.at[3, own_x], dy=UP)
    a_dn = send(S.at[0, own_x], S.at[1, own_x], dy=DOWN)
    sx.wait_recv()
    b_up = send(S.at[0, far_x], S.at[3, far_x], dy=UP)
    b_dn = send(S.at[0, far_x], S.at[1, far_x], dy=DOWN)

    q_dn.wait_recv()
    q_dn2 = send(pblock(1, UP), pblock(1, UP), dz=DOWN)
    p_sib.append(send(pblock(1, UP), pblock(1, UP), dk=1))
    q_up.wait_recv()
    p_sib.append(send(pblock(1, DOWN), pblock(1, DOWN), dk=1))
    w_up2.wait_recv()
    w_dn2.wait_recv()
    w_sib.append(send(wslab(2), wslab(2), dk=1))
    p_up2.wait_recv()
    p_sib.append(send(pblock(0, 2), pblock(0, 2), dk=1))
    q_dn2.wait_recv()
    p_sib.append(send(pblock(1, 2), pblock(1, 2), dk=1))

    for copy in w_sib:
        copy.wait_recv()
    t_up2.wait_recv()
    t_dn2.wait_recv()

    def product(rows, col0, n):
        cols = pl.ds(pl.multiple_of(col0 + 256 * n, 256), 256)
        w = W[:, :, cols].reshape(2048, 256)
        return jnp.dot(T[rows, :], w, preferred_element_type=F32)

    rs_t = []
    for q in range(4):
        rows = pl.ds(256 * q, 256)

        @pl.loop(0, 4)
        def _(n):
            cols = pl.ds(pl.multiple_of(256 * n, 256), 256)
            psend[rows, cols] = product(rows, 1024 * (1 - xl), n).astype(BF16)

        rs_t.append(send(psend.at[rows], precv.at[rows], dxl=1))

    a_up.wait_recv()
    a_up2 = send(S.at[3, own_x], S.at[2, own_x], dy=UP)

    l_res.wait()
    for q in range(4):
        rows = pl.ds(256 * q, 256)

        @pl.loop(0, 4)
        def _(n):
            cols = pl.ds(pl.multiple_of(256 * n, 256), 256)
            H[rows, cols] = product(rows, 1024 * xl, n) + R[rows, cols].astype(F32)

    b_dn.wait_recv()
    b_dn2 = send(S.at[1, far_x], S.at[2, far_x], dy=DOWN)

    def mapped(r):
        @pl.loop(0, 4)
        def _(n):
            cols = pl.ds(pl.multiple_of(256 * n, 256), 256)
            M[pl.ds(256 * r, 256), cols] = jnp.dot(
                S[r], PR[:, cols], preferred_element_type=F32
            )

    for copy in p_sib:
        copy.wait_recv()
    sxy[0].wait_recv()
    mapped(0)

    for q in range(4):
        rs_t[q].wait_recv()

        @pl.loop(0, 16)
        def _(i):
            rows = pl.ds(pl.multiple_of(256 * q + 16 * i, 16), 16)
            h = H[rows, :] + precv[rows, :].astype(F32)
            H[rows, :] = h
            col[rows, :] = jnp.broadcast_to(jnp.sum(h * h, axis=1, keepdims=True), (16, 128))

    sq[0] = col[...].T[0:8, :]
    sq_c = [send(sq.at[0], sq.at[dy * 2 + dx], dy=dy, dxl=dx) for dy, dx in TENSOR]

    a_dn.wait_recv()
    b_up.wait_recv()
    sxy[1].wait_recv()
    mapped(3)
    sxy[2].wait_recv()
    mapped(1)

    for copy in sq_c:
        copy.wait_recv()
    total = sq[0]
    for i in range(1, 8):
        total = total + sq[i]
    inv = lax.rsqrt(total * (1.0 / 8192) + EPS)
    col[...] = jnp.broadcast_to(inv[0:1, :], (128, 1024)).T

    gains = tea_gain[:, pl.ds(pl.multiple_of(1024 * t, 1024), 1024)]

    def errors(r, acc):
        for b in range(2):
            base = 128 * (2 * ((y + r) % 4) + (xl + b) % 2)

            def step(i, acc):
                there = pl.ds(pl.multiple_of(base + 16 * i, 16), 16)
                here = pl.ds(pl.multiple_of(256 * r + 128 * b + 16 * i, 16), 16)
                scale = jnp.concatenate([col[there, :]] * 8, axis=1)
                e = M[here, :] - H[there, :] * scale * gains
                E[here, :] = e.astype(BF16)
                return acc + fold(jnp.add, e * e)

            acc = lax.fori_loop(0, 8, step, acc)
        return acc

    acc = jnp.zeros((8, 128), F32)
    for r in (0, 3, 1):
        acc = errors(r, acc)
    a_up2.wait_recv()
    b_dn2.wait_recv()
    sxy[3].wait_recv()
    mapped(2)
    acc = errors(2, acc)

    row = lax.broadcasted_iota(jnp.int32, (8, 128), 0)
    tile = jnp.where(row == 0, jnp.max(amax_in), jnp.where(row == 1, jnp.max(amax_w), jnp.sum(acc)))

    def merge(first, count):
        out = scal[first]
        for i in range(1, count):
            v = scal[first + i]
            out = jnp.where(row < 2, jnp.maximum(out, v), out + v)
        return out

    scal[t] = tile
    sc1 = [send(scal.at[t], scal.at[t], dy=dy, dxl=dx) for dy, dx in TENSOR]

    for copy in w_up, w_dn, w_up2, w_dn2, *w_sib:
        copy.wait_send()

    def gslot(g, other):
        return W.at[g // 2, pl.ds(256 * (g % 2), 256), pl.ds(1024 * other, 1024)]

    def term(g, dxh, dz, other):
        dest = ((xh + dxh) % 2) * 8 + ((z + dz) % 4) * 2 + (k + other) % 2
        cols = pl.ds(pl.multiple_of(256 * dest, 256), 256)
        st[...] = S[:, :, cols].reshape(1024, 256).T

        @pl.loop(0, 4)
        def _(n):
            at = pl.multiple_of(256 * n, 256)
            W[g // 2, pl.ds(256 * (g % 2), 256), pl.ds(pl.multiple_of(1024 * other + at, 256), 256)] = jnp.dot(
                st[...], E[:, pl.ds(at, 256)], preferred_element_type=F32
            ).astype(BF16)

    ORDER = [(1, 2), (1, 1), (1, 3), (0, 2), (1, 0), (0, 1), (0, 3), (0, 0)]
    to_sib, out_c = [], []

    def finish(g):
        dxh, dz = ORDER[g]
        to_sib[g].wait_recv()

        @pl.loop(0, 16)
        def _(i):
            rows = pl.ds(pl.multiple_of(256 * (g % 2) + 16 * i, 16), 16)
            from_sib = sib[g, pl.ds(pl.multiple_of(16 * i, 16), 16), :].astype(F32)
            both = W[g // 2, rows, pl.ds(0, 1024)].astype(F32) + from_sib
            W[g // 2, rows, pl.ds(0, 1024)] = both.astype(BF16)

        if g < 7:
            out_c.append(send(gslot(g, 0), rs.at[g], dxh=dxh, dz=dz))

    sc2 = None
    for g, (dxh, dz) in enumerate(ORDER):
        term(g, dxh, dz, 1)
        to_sib.append(send(gslot(g, 1), sib.at[g], dk=1))
        term(g, dxh, dz, 0)
        if g > 0:
            finish(g - 1)
        if g == 3:
            for copy in sc1:
                copy.wait_recv()
            at = 8 + xh * 4 + z
            scal[at] = merge(0, 8)
            sc2 = [send(scal.at[at], scal.at[at], dxh=dx, dz=dz_) for dx, dz_ in CONTEXT]
    finish(7)

    for copy in sc2:
        copy.wait_recv()
    scal[16 + k] = merge(8, 8)
    sc3 = send(scal.at[16 + k], scal.at[16 + k], dk=1)

    for copy in out_c:
        copy.wait_recv()
    scale = 1.0 / math.sqrt(tokens_all)

    @pl.loop(0, 16)
    def _(i):
        rows = pl.ds(pl.multiple_of(16 * i, 16), 16)
        total = W[3, pl.ds(pl.multiple_of(256 + 16 * i, 16), 16), pl.ds(0, 1024)].astype(F32)
        for g in range(7):
            total = total + rs[g, rows, :].astype(F32)
        grad[rows, :] = total * scale

    sc3.wait_recv()
    final = merge(16, 2)
    hist_in_new[0] = jnp.max(jnp.where(row == 0, final, 0.0))
    hist_w_new[0] = jnp.max(jnp.where(row == 1, final, 0.0))
    loss[0] = jnp.max(jnp.where(row == 2, final, 0.0)) * (0.5 / (tokens_all * 8192))
    for i in range(15):
        hist_in_new[i + 1] = hist_in[i]
        hist_w_new[i + 1] = hist_w[i]

    waited = [w_up, w_dn, w_up2, w_dn2, *w_sib]
    for copy in sends:
        if not any(copy is w for w in waited):
            copy.wait_send()


def local(
    teacher_in, teacher_resid, teacher_wo, teacher_gain, input_history, weight_history,
    student_hidden, student_gain, projection,
):
    tokens_all = teacher_in.shape[0] * lax.axis_size("context")
    smem = pl.BlockSpec(memory_space=pltpu.SMEM)
    vmem = pl.BlockSpec(memory_space=pltpu.VMEM)
    hbm = pl.BlockSpec(memory_space=pl.ANY)
    grad, hist_in, hist_w, loss = pl.pallas_call(
        functools.partial(kernel, tokens_all),
        name="distill",
        out_shape=(
            jax.ShapeDtypeStruct((256, 1024), F32),
            jax.ShapeDtypeStruct((16,), F32),
            jax.ShapeDtypeStruct((16,), F32),
            jax.ShapeDtypeStruct((1,), F32),
        ),
        in_specs=[smem, smem, vmem, vmem, hbm, hbm, hbm, hbm, hbm],
        out_specs=(vmem, smem, smem, smem),
        scratch_shapes=[
            pltpu.VMEM((1024, 2048), BF16),
            pltpu.VMEM((4, 512, 2048), BF16),
            pltpu.VMEM((4, 256, 4096), BF16),
            pltpu.VMEM((4096, 1024), BF16),
            pltpu.VMEM((1024, 1024), BF16),
            pltpu.VMEM((1024, 1024), F32),
            pltpu.VMEM((1024, 1024), F32),
            pltpu.VMEM((1024, 1024), BF16),
            pltpu.VMEM((1024, 1024), BF16),
            pltpu.VMEM((1024, 1024), BF16),
            pltpu.VMEM((128, 4096), BF16),
            pltpu.VMEM((64, 8192), BF16),
            pltpu.VMEM((1024, 128), F32),
            pltpu.VMEM((8, 8, 1024), F32),
            pltpu.VMEM((18, 8, 128), F32),
            pltpu.VMEM((8, 256, 1024), BF16),
            pltpu.VMEM((7, 256, 1024), BF16),
            pltpu.VMEM((256, 1024), BF16),
            pltpu.SemaphoreType.DMA((COPIES,)),
            pltpu.SemaphoreType.DMA((COPIES,)),
            pltpu.SemaphoreType.DMA((6,)),
        ],
        compiler_params=pltpu.CompilerParams(
            collective_id=0, has_side_effects=True, vmem_limit_bytes=62 << 20
        ),
        cost_estimate=pl.CostEstimate(
            flops=3 * 2 * 1024 * 1024 * 4096, bytes_accessed=16 << 20, transcendentals=1024
        ),
    )(
        input_history,
        weight_history,
        student_gain.reshape(1, -1),
        teacher_gain.reshape(1, -1),
        teacher_in,
        teacher_resid,
        teacher_wo,
        student_hidden,
        projection,
    )
    return grad, loss.reshape(()), hist_in, hist_w


def solution(mesh):
    placed = (
        P("context", "tensor"),
        P("context", "tensor"),
        P("tensor", None),
        P(),
        P(),
        P(),
        P(("context", "tensor"), None),
        P(),
        P("context", "tensor"),
    )
    return jax.shard_map(
        local,
        mesh=mesh,
        in_specs=placed,
        out_specs=(P("context", "tensor"), P(), P(), P()),
        check_vma=False,
    )
```

time: 806 us -> 203 us (0.25)
  waiting for transfers between devices: 553 us -> 0 us
  Pallas kernels: 0 us -> 195 us
  blocking collectives: 172 us -> 0 us
  matrix products: 43.1 us -> 0 us
  other arithmetic: 16.9 us -> 0 us
  between operations: 16.9 us -> 2.41 us
    reduce_scatter x2 -> x0, waiting for transfers between devices: 325 us -> none  [the longest x1 325 us: local(): lax.psum_scatter(partial_value.astype(jnp.bfloat16), 'tensor', scatter_di...]
    all_gather x2 -> x0, waiting for transfers between devices: 227 us -> none  [the longest x1 151 us: local(): group_rows = lax.all_gather(student_norm, 'tensor', axis=0, tiled=True)]
    pallas_call x0 -> x1, Pallas kernels: none -> 195 us  [local(): pl.pallas_call(functools.partial(kernel, tokens_all), name='distill', out...]
    pmax x2 -> x0, blocking collectives: 90.2 us -> none  [the longest x1 71.9 us: local(): input_amax = lax.pmax(local_input, ('tensor', 'context'))]
    psum x2 -> x0, blocking collectives: 81.8 us -> none  [the longest x1 62.9 us: local(): error_sum = lax.psum(jnp.sum(error * error), ('tensor', 'context'))]
    dot_general x3 -> x0, matrix products: 43.1 us -> none  [the longest x1 16.1 us: local(): jnp.dot(input_sat, weight_sat, preferred_element_type=jnp.float32)]
    reduce_max x4 -> x0, other arithmetic: 8.42 us -> none  [the longest x1 5.16 us: local(): local_weight = jnp.max(jnp.abs(teacher_wo.astype(jnp.float32)))]
  transfers between devices with their start and end apart: 4 -> 0, of which waited for: 3 -> 0; matrix products, arithmetic and copies ran while one was open for 2% -> 0% of each run, Pallas kernels for 0% -> 0%
where the time goes in v1:
time: 203 us; the launch traced here: 202 us
  Pallas kernels  195 us (96%)
  local copies, waits for them, and re-layouts  4.56 us (2%)
  between operations  2.41 us (1%)
    pallas_call x1, Pallas kernels, local(): pl.pallas_call(functools.partial(kernel, tokens_all), name='distill', out...  195 us
    unnamed x3, local copies, waits for them, and re-layouts  4.56 us

profile of v1, /device:TPU:0, one launch (start us, length us, event | category | flops | bytes accessed | tf_op | source)
XLA Modules:
  0.0 202.2 jit_solution(205479768802659545)
XLA Ops:
  0.6 195.2 %distill.1 = (f32[256,1024]{1,0:T(8,128)}, f32[16]{0:T(128)}, f32[16]{0:T(128)}, f32[1]{0:T(128)}) custom-call(f32[16]{0:T(128)} %hist_in.1, f32[16]{0:T(128)} %hist_w.1, f32[1,4096]{1,0:T(1,128)} %bitcast.4, f32[1,8192]{1,0:T(1,128)} %bitcast.3, bf16[1024,512]{1,0:T(8,128)(2,1)} %tin.1, bf16[1024,1024]{1,0:T(8,128)(2,1)} %resid.1, bf16[512,8192]{1,0:T(8,128)(2,1)} %wo.1, ...), custom_call_target="tpu_custom_call" | custom-call | flops 25769803776 | bytes 16777216 | tf_op jit(solution)/shard_map/distill/pallas_call | solution.py:446
  195.8 2.3 %copy.17 = f32[256,1024]{1,0:T(8,128)} copy(f32[256,1024]{1,0:T(8,128)} %get-tuple-element.16) | data formatting | bytes 2097152
  198.8 1.1 copy.19
  199.9 1.1 copy.20

commit v2 on v1

--- a/solution.py
+++ b/solution.py
@@ -12,7 +12,8 @@
 F32, BF16 = jnp.float32, jnp.bfloat16
 EPS = 1e-05
 COPIES = 100
-XROWS = 80
+XROWS = 96
+ACOLS = 640
 
 
 def lanes(tile):
@@ -37,7 +38,7 @@
     tokens_all,
     hist_in, hist_w, stu_gain, tea_gain, tin, resid, wo, stu, proj,
     grad, hist_in_new, hist_w_new, loss,
-    T, W, S, PR, R, H, M, E, psend, precv, sraw, wraw, col, sq, scal, sib, rs, st,
+    T, W, S, PR, R, H, M, E, psend, precv, sraw, wraw, col, sq, scal, sib, ra1, ra2, rb1, rb2, st,
     ssem, rsem, lsem,
 ):
     t, c = lax.axis_index("tensor"), lax.axis_index("context")
@@ -77,11 +78,10 @@
     CONTEXT = [(dx, dz) for dx in range(2) for dz in range(4) if (dx, dz) != (0, 0)]
     UP, DOWN = 1, 3
 
-    j_own = 2 * z + k
-    slab = pl.multiple_of(64 * j_own, 64)
+    slab = pl.multiple_of(64 * (2 * z + k), 64)
+    l_wraw = load(wo.at[pl.ds(slab, 64)], wraw)
+    l_stu = load(stu, sraw)
     l_proj = load(proj, PR.at[pl.ds(pl.multiple_of(256 * c, 256), 256)])
-    l_stu = load(stu, sraw)
-    l_wraw = load(wo.at[pl.ds(slab, 64)], wraw)
     l_tin = load(tin, T.at[:, pl.ds(0, 512)])
     l_wown = load(wo.at[:, pl.ds(pl.multiple_of(2048 * y, 2048), 2048)], W.at[0])
     l_res = load(resid, R)
@@ -97,36 +97,6 @@
     for i in range(1, 16):
         lim_in = jnp.maximum(lim_in, hist_in[i])
         lim_w = jnp.maximum(lim_w, hist_w[i])
-
-    l_stu.wait()
-
-    @pl.loop(0, 8)
-    def _(i):
-        rows = pl.ds(pl.multiple_of(16 * i, 16), 16)
-        v = sraw[rows, :].astype(F32)
-        mean = jnp.mean(v * v, axis=1, keepdims=True)
-        S[0, rows, :] = (v * lax.rsqrt(mean + EPS) * stu_gain[...]).astype(BF16)
-
-    pl.semaphore_wait(barrier, len(TENSOR) + len(CONTEXT) + 1)
-
-    nx = XROWS
-    ny = 128 - nx
-    own_x, own_y = pl.ds(0, nx), pl.ds(nx, ny)
-    far_x, far_y = pl.ds(128, nx), pl.ds(128 + nx, ny)
-    sy_up = send(S.at[0, own_y], S.at[3, own_y], dy=UP)
-    sy_dn = send(S.at[0, own_y], S.at[1, own_y], dy=DOWN)
-    l_proj.wait()
-
-    def pblock(dxh=0, dz=0):
-        at = ((xh + dxh) % 2) * 8 + ((z + dz) % 4) * 2 + k
-        return PR.at[pl.ds(pl.multiple_of(256 * at, 256), 256)]
-
-    p_x = send(pblock(), pblock(), dxh=1)
-    p_up = send(pblock(), pblock(), dz=UP)
-    p_dn = send(pblock(), pblock(), dz=DOWN)
-    p_sib = [send(pblock(), pblock(), dk=1)]
-    sx = send(S.at[0, own_x], S.at[0, far_x], dxl=1)
-    sxy = [send(S.at[0, own_y], S.at[0, far_y], dxl=1)]
 
     l_wraw.wait()
 
@@ -141,12 +111,42 @@
 
     amax_w = lax.fori_loop(0, 4, clip_w, jnp.zeros((8, 128), F32))
 
+    l_stu.wait()
+
+    @pl.loop(0, 8)
+    def _(i):
+        rows = pl.ds(pl.multiple_of(16 * i, 16), 16)
+        v = sraw[rows, :].astype(F32)
+        mean = jnp.mean(v * v, axis=1, keepdims=True)
+        S[0, rows, :] = (v * lax.rsqrt(mean + EPS) * stu_gain[...]).astype(BF16)
+
+    pl.semaphore_wait(barrier, len(TENSOR) + len(CONTEXT) + 1)
+
+    nx = XROWS
+    ny = 128 - nx
+    own_x, own_y = pl.ds(0, nx), pl.ds(nx, ny)
+    far_x, far_y = pl.ds(128, nx), pl.ds(128 + nx, ny)
+    sy_up = send(S.at[0, own_y], S.at[3, own_y], dy=UP)
+    sy_dn = send(S.at[0, own_y], S.at[1, own_y], dy=DOWN)
+
     def wcols(d):
         return pl.ds(pl.multiple_of(2048 * ((y + d) % 4), 2048), 2048)
 
     w_y = [
-        send(wraw.at[:, wcols(d)], W.at[4 - d, pl.ds(slab, 64)], dy=d) for d in (1, 3, 2)
+        send(wraw.at[:, wcols(d)], W.at[4 - d, pl.ds(slab, 64)], dy=d) for d in (2, 1, 3)
     ]
+    l_proj.wait()
+
+    def pblock(dxh=0, dz=0):
+        at = ((xh + dxh) % 2) * 8 + ((z + dz) % 4) * 2 + k
+        return PR.at[pl.ds(pl.multiple_of(256 * at, 256), 256)]
+
+    p_x = send(pblock(), pblock(), dxh=1)
+    p_up = send(pblock(), pblock(), dz=UP)
+    p_dn = send(pblock(), pblock(), dz=DOWN)
+    p_sib = [send(pblock(), pblock(), dk=1)]
+    sx = send(S.at[0, own_x], S.at[0, far_x], dxl=1)
+    sxy = [send(S.at[0, own_y], S.at[0, far_y], dxl=1)]
 
     l_tin.wait()
 
@@ -157,12 +157,6 @@
         return jnp.maximum(amax, fold(jnp.maximum, jnp.abs(v)))
 
     amax_in = lax.fori_loop(0, 32, clip_t, jnp.zeros((8, 128), F32))
-
-    def tblock(r, rows=None):
-        return T.at[pl.ds(0, 1024) if rows is None else rows, pl.ds(512 * r, 512)]
-
-    t_up = send(tblock(0), tblock(3), dy=UP)
-    t_dn = send(tblock(0), tblock(1), dy=DOWN)
 
     left, right = pl.ds(0, 2048), pl.ds(2048, 2048)
     sy_up.wait_recv()
@@ -172,10 +166,15 @@
     sy_dn2 = send(S.at[1, own_y, right], S.at[2, own_y, right], dy=DOWN)
     sxy.append(send(S.at[1, own_y], S.at[1, far_y], dxl=1))
 
-    p_x.wait_recv()
-    q_up = send(pblock(1), pblock(1), dz=UP)
-    q_dn = send(pblock(1), pblock(1), dz=DOWN)
-    p_sib.append(send(pblock(1), pblock(1), dk=1))
+    low, high = pl.ds(0, 512), pl.ds(512, 512)
+
+    def tblock(r, rows):
+        return T.at[rows, pl.ds(512 * r, 512)]
+
+    t_up = send(tblock(0, low), tblock(3, low), dy=UP)
+    t_dn = send(tblock(0, high), tblock(1, high), dy=DOWN)
+    t_up1 = send(tblock(0, high), tblock(3, high), dy=UP)
+    t_dn1 = send(tblock(0, low), tblock(1, low), dy=DOWN)
 
     def wslab(dz=0, half=None):
         at = pl.multiple_of(64 * (2 * ((z + dz) % 4) + k), 64)
@@ -183,6 +182,8 @@
             return W.at[pl.ds(1, 3), pl.ds(at, 64)]
         return W.at[pl.ds(1, 3), pl.ds(pl.multiple_of(at + 32 * half, 32), 32)]
 
+    p_x.wait_recv()
+    p_sib.append(send(pblock(1), pblock(1), dk=1))
     for copy in w_y:
         copy.wait_recv()
     w_up = send(wslab(), wslab(), dz=UP)
@@ -197,14 +198,19 @@
         v = W[0, rows, :].astype(F32)
         W[0, rows, :] = jnp.clip(v, -lim_w, lim_w).astype(BF16)
 
-    p_up.wait_recv()
-    p_up2 = send(pblock(0, DOWN), pblock(0, DOWN), dz=UP)
-    p_sib.append(send(pblock(0, DOWN), pblock(0, DOWN), dk=1))
-    p_dn.wait_recv()
-    p_sib.append(send(pblock(0, UP), pblock(0, UP), dk=1))
     sy_up2.wait_recv()
     sy_dn2.wait_recv()
     sxy.append(send(S.at[2, own_y], S.at[2, far_y], dxl=1))
+
+    t_up.wait_recv()
+    t_up2 = send(tblock(3, low), tblock(2, low), dy=UP)
+    t_dn.wait_recv()
+    t_dn2 = send(tblock(1, high), tblock(2, high), dy=DOWN)
+    a_up = send(S.at[0, own_x], S.at[3, own_x], dy=UP)
+    sx.wait_recv()
+    b_dn = send(S.at[0, far_x], S.at[1, far_x], dy=DOWN)
+    b_up = send(S.at[0, far_x], S.at[3, far_x], dy=UP)
+    a_dn = send(S.at[0, own_x], S.at[1, own_x], dy=DOWN)
 
     w_up.wait_recv()
     w_up2 = send(wslab(DOWN, 0), wslab(DOWN, 0), dz=UP)
@@ -212,64 +218,57 @@
     w_dn.wait_recv()
     w_dn2 = send(wslab(UP, 1), wslab(UP, 1), dz=DOWN)
     w_sib.append(send(wslab(UP), wslab(UP), dk=1))
-
-    t_up.wait_recv()
-    t_up2 = send(tblock(3, pl.ds(0, 512)), tblock(2, pl.ds(0, 512)), dy=UP)
-    t_dn.wait_recv()
-    t_dn2 = send(tblock(1, pl.ds(512, 512)), tblock(2, pl.ds(512, 512)), dy=DOWN)
-
-    a_up = send(S.at[0, own_x], S.at[3, own_x], dy=UP)
-    a_dn = send(S.at[0, own_x], S.at[1, own_x], dy=DOWN)
-    sx.wait_recv()
-    b_up = send(S.at[0, far_x], S.at[3, far_x], dy=UP)
-    b_dn = send(S.at[0, far_x], S.at[1, far_x], dy=DOWN)
-
-    q_dn.wait_recv()
-    q_dn2 = send(pblock(1, UP), pblock(1, UP), dz=DOWN)
-    p_sib.append(send(pblock(1, UP), pblock(1, UP), dk=1))
-    q_up.wait_recv()
-    p_sib.append(send(pblock(1, DOWN), pblock(1, DOWN), dk=1))
+    q_dn = send(pblock(1), pblock(1), dz=DOWN)
+    q_up = send(pblock(1), pblock(1), dz=UP)
+    p_up.wait_recv()
+    p_up2 = send(pblock(0, DOWN), pblock(0, DOWN), dz=UP)
+    p_sib.append(send(pblock(0, DOWN), pblock(0, DOWN), dk=1))
+    p_dn.wait_recv()
+    p_sib.append(send(pblock(0, UP), pblock(0, UP), dk=1))
     w_up2.wait_recv()
     w_dn2.wait_recv()
     w_sib.append(send(wslab(2), wslab(2), dk=1))
+
+    for copy in t_up1, t_dn1, t_up2, t_dn2, *w_sib:
+        copy.wait_recv()
+
+    def product(rows, col0, n):
+        cols = pl.ds(pl.multiple_of(col0 + 256 * n, 256), 256)
+        w = W[:, :, cols].reshape(2048, 256)
+        return jnp.dot(T[rows, :], w, preferred_element_type=F32)
+
+    rs_t = []
+    for q in range(4):
+        rows = pl.ds(256 * q, 256)
+
+        @pl.loop(0, 4)
+        def _(n):
+            cols = pl.ds(pl.multiple_of(256 * n, 256), 256)
+            psend[rows, cols] = product(rows, 1024 * (1 - xl), n).astype(BF16)
+
+        rs_t.append(send(psend.at[rows], precv.at[rows], dxl=1))
+        if q == 1:
+            q_dn.wait_recv()
+            q_dn2 = send(pblock(1, UP), pblock(1, UP), dz=DOWN)
+            p_sib.append(send(pblock(1, UP), pblock(1, UP), dk=1))
+            q_up.wait_recv()
+            p_sib.append(send(pblock(1, DOWN), pblock(1, DOWN), dk=1))
+
+    l_res.wait()
+    for q in range(4):
+        rows = pl.ds(256 * q, 256)
+
+        @pl.loop(0, 4)
+        def _(n):
+            cols = pl.ds(pl.multiple_of(256 * n, 256), 256)
+            H[rows, cols] = product(rows, 1024 * xl, n) + R[rows, cols].astype(F32)
+
     p_up2.wait_recv()
     p_sib.append(send(pblock(0, 2), pblock(0, 2), dk=1))
     q_dn2.wait_recv()
     p_sib.append(send(pblock(1, 2), pblock(1, 2), dk=1))
-
-    for copy in w_sib:
-        copy.wait_recv()
-    t_up2.wait_recv()
-    t_dn2.wait_recv()
-
-    def product(rows, col0, n):
-        cols = pl.ds(pl.multiple_of(col0 + 256 * n, 256), 256)
-        w = W[:, :, cols].reshape(2048, 256)
-        return jnp.dot(T[rows, :], w, preferred_element_type=F32)
-
-    rs_t = []
-    for q in range(4):
-        rows = pl.ds(256 * q, 256)
-
-        @pl.loop(0, 4)
-        def _(n):
-            cols = pl.ds(pl.multiple_of(256 * n, 256), 256)
-            psend[rows, cols] = product(rows, 1024 * (1 - xl), n).astype(BF16)
-
-        rs_t.append(send(psend.at[rows], precv.at[rows], dxl=1))
-
     a_up.wait_recv()
     a_up2 = send(S.at[3, own_x], S.at[2, own_x], dy=UP)
-
-    l_res.wait()
-    for q in range(4):
-        rows = pl.ds(256 * q, 256)
-
-        @pl.loop(0, 4)
-        def _(n):
-            cols = pl.ds(pl.multiple_of(256 * n, 256), 256)
-            H[rows, cols] = product(rows, 1024 * xl, n) + R[rows, cols].astype(F32)
-
     b_dn.wait_recv()
     b_dn2 = send(S.at[1, far_x], S.at[2, far_x], dy=DOWN)
 
@@ -281,12 +280,7 @@
                 S[r], PR[:, cols], preferred_element_type=F32
             )
 
-    for copy in p_sib:
-        copy.wait_recv()
-    sxy[0].wait_recv()
-    mapped(0)
-
-    for q in range(4):
+    def squares(q):
         rs_t[q].wait_recv()
 
         @pl.loop(0, 16)
@@ -296,16 +290,22 @@
             H[rows, :] = h
             col[rows, :] = jnp.broadcast_to(jnp.sum(h * h, axis=1, keepdims=True), (16, 128))
 
-    sq[0] = col[...].T[0:8, :]
-    sq_c = [send(sq.at[0], sq.at[dy * 2 + dx], dy=dy, dxl=dx) for dy, dx in TENSOR]
-
-    a_dn.wait_recv()
+    for copy in p_sib:
+        copy.wait_recv()
+    sxy[0].wait_recv()
+    mapped(0)
+    squares(0)
+    squares(1)
+    squares(2)
     b_up.wait_recv()
     sxy[1].wait_recv()
     mapped(3)
+    a_dn.wait_recv()
     sxy[2].wait_recv()
     mapped(1)
-
+    squares(3)
+    sq[0] = col[...].T[0:8, :]
+    sq_c = [send(sq.at[0], sq.at[dy * 2 + dx], dy=dy, dxl=dx) for dy, dx in TENSOR]
     for copy in sq_c:
         copy.wait_recv()
     total = sq[0]
@@ -356,69 +356,106 @@
     for copy in w_up, w_dn, w_up2, w_dn2, *w_sib:
         copy.wait_send()
 
-    def gslot(g, other):
-        return W.at[g // 2, pl.ds(256 * (g % 2), 256), pl.ds(1024 * other, 1024)]
-
-    def term(g, dxh, dz, other):
-        dest = ((xh + dxh) % 2) * 8 + ((z + dz) % 4) * 2 + (k + other) % 2
-        cols = pl.ds(pl.multiple_of(256 * dest, 256), 256)
-        st[...] = S[:, :, cols].reshape(1024, 256).T
+    ORDER = [(1, 2), (0, 2), (1, 1), (0, 1), (1, 3), (0, 3), (1, 0), (0, 0)]
+    a_cols, b_cols = pl.ds(0, ACOLS), pl.ds(ACOLS, 1024 - ACOLS)
+
+    def gslot(dxh, dz, cols):
+        g = ORDER.index((dxh, dz))
+        return W.at[g // 2, pl.ds(256 * (g % 2), 256), cols]
+
+    to_sib, a_1, b_1, a_2 = [], {}, {}, {}
+
+    def term(g):
+        dxh, dz = ORDER[g]
+        chip = ((xh + dxh) % 2) * 4 + (z + dz) % 4
+        for other in (1, 0):
+            cols = pl.ds(pl.multiple_of(512 * chip + 256 * ((k + other) % 2), 256), 256)
+            st[pl.ds(256 * (1 - other), 256), :] = S[:, :, cols].reshape(1024, 256).T
 
         @pl.loop(0, 4)
         def _(n):
             at = pl.multiple_of(256 * n, 256)
-            W[g // 2, pl.ds(256 * (g % 2), 256), pl.ds(pl.multiple_of(1024 * other + at, 256), 256)] = jnp.dot(
-                st[...], E[:, pl.ds(at, 256)], preferred_element_type=F32
-            ).astype(BF16)
-
-    ORDER = [(1, 2), (1, 1), (1, 3), (0, 2), (1, 0), (0, 1), (0, 3), (0, 0)]
-    to_sib, out_c = [], []
+            both = jnp.dot(st[...], E[:, pl.ds(at, 256)], preferred_element_type=F32).astype(BF16)
+            rows = pl.ds(256 * (g % 2), 256)
+            W[g // 2, rows, pl.ds(pl.multiple_of(1024 + at, 256), 256)] = both[:256]
+            W[g // 2, rows, pl.ds(at, 256)] = both[256:]
+
+        to_sib.append(send(gslot(dxh, dz, pl.ds(1024, 1024)), sib.at[g], dk=1))
+
+    def add(dxh, dz, start, count, others):
+        g = ORDER.index((dxh, dz))
+
+        @pl.loop(0, 16)
+        def _(i):
+            here = pl.ds(pl.multiple_of(16 * i, 16), 16)
+            rows = pl.ds(pl.multiple_of(256 * (g % 2) + 16 * i, 16), 16)
+            cols = pl.ds(start, count)
+            total = W[g // 2, rows, cols].astype(F32)
+            for ref, index in others:
+                total = total + ref[index, here, :].astype(F32)
+            W[g // 2, rows, cols] = total.astype(BF16)
 
     def finish(g):
         dxh, dz = ORDER[g]
         to_sib[g].wait_recv()
-
-        @pl.loop(0, 16)
-        def _(i):
-            rows = pl.ds(pl.multiple_of(256 * (g % 2) + 16 * i, 16), 16)
-            from_sib = sib[g, pl.ds(pl.multiple_of(16 * i, 16), 16), :].astype(F32)
-            both = W[g // 2, rows, pl.ds(0, 1024)].astype(F32) + from_sib
-            W[g // 2, rows, pl.ds(0, 1024)] = both.astype(BF16)
-
-        if g < 7:
-            out_c.append(send(gslot(g, 0), rs.at[g], dxh=dxh, dz=dz))
-
-    sc2 = None
-    for g, (dxh, dz) in enumerate(ORDER):
-        term(g, dxh, dz, 1)
-        to_sib.append(send(gslot(g, 1), sib.at[g], dk=1))
-        term(g, dxh, dz, 0)
-        if g > 0:
-            finish(g - 1)
-        if g == 3:
+        add(dxh, dz, 0, 1024, [(sib, g)])
+        if dxh:
+            a_1[dz] = send(gslot(dxh, dz, a_cols), ra1.at[dz], dxh=1)
+        if dz:
+            b_1[dxh, dz] = send(gslot(dxh, dz, b_cols), rb1.at[dxh * 3 + dz - 1], dz=dz)
+
+    def second_a(dz):
+        a_1[dz].wait_recv()
+        add(0, dz, 0, ACOLS, [(ra1, dz)])
+        if dz:
+            a_2[dz] = send(gslot(0, dz, a_cols), ra2.at[dz - 1], dz=dz)
+
+    for g in range(8):
+        term(g)
+        if g == 1:
             for copy in sc1:
                 copy.wait_recv()
             at = 8 + xh * 4 + z
             scal[at] = merge(0, 8)
-            sc2 = [send(scal.at[at], scal.at[at], dxh=dx, dz=dz_) for dx, dz_ in CONTEXT]
+            sc2 = [send(scal.at[at], scal.at[at], dxh=dx, dz=dz) for dx, dz in CONTEXT]
+        if g:
+            finish(g - 1)
+        if g == 4:
+            second_a(2)
+        if g == 6:
+            second_a(1)
     finish(7)
+    second_a(3)
 
     for copy in sc2:
         copy.wait_recv()
     scal[16 + k] = merge(8, 8)
     sc3 = send(scal.at[16 + k], scal.at[16 + k], dk=1)
 
-    for copy in out_c:
-        copy.wait_recv()
+    for dz in (1, 2, 3):
+        b_1[1, dz].wait_recv()
+    add(1, 0, ACOLS, 1024 - ACOLS, [(rb1, 3), (rb1, 4), (rb1, 5)])
+    b_2 = send(gslot(1, 0, b_cols), rb2.at[0], dxh=1)
+    second_a(0)
+
+    for dz in (1, 2, 3):
+        b_1[0, dz].wait_recv()
+        a_2[dz].wait_recv()
+    b_2.wait_recv()
     scale = 1.0 / math.sqrt(tokens_all)
 
     @pl.loop(0, 16)
     def _(i):
         rows = pl.ds(pl.multiple_of(16 * i, 16), 16)
-        total = W[3, pl.ds(pl.multiple_of(256 + 16 * i, 16), 16), pl.ds(0, 1024)].astype(F32)
-        for g in range(7):
-            total = total + rs[g, rows, :].astype(F32)
-        grad[rows, :] = total * scale
+        mine = pl.ds(pl.multiple_of(256 + 16 * i, 16), 16)
+        total = W[3, mine, a_cols].astype(F32)
+        for n in range(3):
+            total = total + ra2[n, rows, :].astype(F32)
+        grad[rows, a_cols] = total * scale
+        total = W[3, mine, b_cols].astype(F32) + rb2[0, rows, :].astype(F32)
+        for n in range(3):
+            total = total + rb1[n, rows, :].astype(F32)
+        grad[rows, b_cols] = total * scale
 
     sc3.wait_recv()
     final = merge(16, 2)
@@ -471,8 +508,11 @@
             pltpu.VMEM((8, 8, 1024), F32),
             pltpu.VMEM((18, 8, 128), F32),
             pltpu.VMEM((8, 256, 1024), BF16),
-            pltpu.VMEM((7, 256, 1024), BF16),
-            pltpu.VMEM((256, 1024), BF16),
+            pltpu.VMEM((4, 256, ACOLS), BF16),
+            pltpu.VMEM((3, 256, ACOLS), BF16),
+            pltpu.VMEM((6, 256, 1024 - ACOLS), BF16),
+            pltpu.VMEM((1, 256, 1024 - ACOLS), BF16),
+            pltpu.VMEM((512, 1024), BF16),
             pltpu.SemaphoreType.DMA((COPIES,)),
             pltpu.SemaphoreType.DMA((COPIES,)),
             pltpu.SemaphoreType.DMA((6,)),

time: 203 us -> 172 us (0.85)
  Pallas kernels: 195 us -> 165 us
    pallas_call x1, Pallas kernels: 195 us -> 165 us  [local(): pl.pallas_call(functools.partial(kernel, tokens_all), name='distill', out...]
where the time goes in v2:
time: 172 us
  Pallas kernels  165 us (96%)
  local copies, waits for them, and re-layouts  4.56 us (3%)
  between operations  2.41 us (1%)
    pallas_call x1, Pallas kernels, local(): pl.pallas_call(functools.partial(kernel, tokens_all), name='distill', out...  165 us
    unnamed x3, local copies, waits for them, and re-layouts  4.56 us

profile of v2, /device:TPU:0, one launch (start us, length us, event | category | flops | bytes accessed | tf_op | source)
XLA Modules:
  0.0 172.2 jit_solution(17295668105921362078)
XLA Ops:
  0.6 165.3 %distill.1 = (f32[256,1024]{1,0:T(8,128)}, f32[16]{0:T(128)}, f32[16]{0:T(128)}, f32[1]{0:T(128)}) custom-call(f32[16]{0:T(128)} %hist_in.1, f32[16]{0:T(128)} %hist_w.1, f32[1,4096]{1,0:T(1,128)} %bitcast.4, f32[1,8192]{1,0:T(1,128)} %bitcast.3, bf16[1024,512]{1,0:T(8,128)(2,1)} %tin.1, bf16[1024,1024]{1,0:T(8,128)(2,1)} %resid.1, bf16[512,8192]{1,0:T(8,128)(2,1)} %wo.1, ...), custom_call_target="tpu_custom_call" | custom-call | flops 25769803776 | bytes 16777216 | tf_op jit(solution)/shard_map/distill/pallas_call | solution.py:483
  165.9 2.3 %copy.17 = f32[256,1024]{1,0:T(8,128)} copy(f32[256,1024]{1,0:T(8,128)} %get-tuple-element.16) | data formatting | bytes 2097152
  168.9 1.1 copy.19
  170.0 1.1 copy.20

commit v3 on v2

--- a/solution.py
+++ b/solution.py
@@ -13,7 +13,7 @@
 EPS = 1e-05
 COPIES = 100
 XROWS = 96
-ACOLS = 640
+ACOLS = 384
 
 
 def lanes(tile):
@@ -37,8 +37,8 @@
 def kernel(
     tokens_all,
     hist_in, hist_w, stu_gain, tea_gain, tin, resid, wo, stu, proj,
-    grad, hist_in_new, hist_w_new, loss,
-    T, W, S, PR, R, H, M, E, psend, precv, sraw, wraw, col, sq, scal, sib, ra1, ra2, rb1, rb2, st,
+    parts,
+    T, W, S, PR, R, H, M, E, psend, precv, sraw, wraw, col, sq, scal, sib, ra1, ra2, rb1, rb2, am, bm, total_g,
     ssem, rsem, lsem,
 ):
     t, c = lax.axis_index("tensor"), lax.axis_index("context")
@@ -158,6 +158,14 @@
 
     amax_in = lax.fori_loop(0, 32, clip_t, jnp.zeros((8, 128), F32))
 
+    low, high = pl.ds(0, 512), pl.ds(512, 512)
+
+    def tblock(r, rows):
+        return T.at[rows, pl.ds(512 * r, 512)]
+
+    t_up = send(tblock(0, low), tblock(3, low), dy=UP)
+    t_dn = send(tblock(0, high), tblock(1, high), dy=DOWN)
+
     left, right = pl.ds(0, 2048), pl.ds(2048, 2048)
     sy_up.wait_recv()
     sy_up2 = send(S.at[3, own_y, left], S.at[2, own_y, left], dy=UP)
@@ -166,13 +174,6 @@
     sy_dn2 = send(S.at[1, own_y, right], S.at[2, own_y, right], dy=DOWN)
     sxy.append(send(S.at[1, own_y], S.at[1, far_y], dxl=1))
 
-    low, high = pl.ds(0, 512), pl.ds(512, 512)
-
-    def tblock(r, rows):
-        return T.at[rows, pl.ds(512 * r, 512)]
-
-    t_up = send(tblock(0, low), tblock(3, low), dy=UP)
-    t_dn = send(tblock(0, high), tblock(1, high), dy=DOWN)
     t_up1 = send(tblock(0, high), tblock(3, high), dy=UP)
     t_dn1 = send(tblock(0, low), tblock(1, low), dy=DOWN)
 
@@ -273,12 +274,31 @@
     b_dn2 = send(S.at[1, far_x], S.at[2, far_x], dy=DOWN)
 
     def mapped(r):
-        @pl.loop(0, 4)
+        @pl.loop(0, 2)
         def _(n):
-            cols = pl.ds(pl.multiple_of(256 * n, 256), 256)
+            cols = pl.ds(pl.multiple_of(512 * n, 512), 512)
             M[pl.ds(256 * r, 256), cols] = jnp.dot(
                 S[r], PR[:, cols], preferred_element_type=F32
             )
+
+    ORDER = [(1, 2), (0, 2), (1, 1), (1, 3), (1, 0), (0, 1), (0, 3), (0, 0)]
+
+    def turned(g):
+        if g < 4:
+            return T, 512 * (g % 2), 1024 * (g // 2)
+        return (R, psend)[g // 2 - 2], 512 * (g % 2), 0
+
+    def turn(g, r):
+        dxh, dz = ORDER[g]
+        chip = ((xh + dxh) % 2) * 4 + (z + dz) % 4
+        ref, row0, col0 = turned(g)
+        for own in (0, 1):
+            cols = pl.ds(pl.multiple_of(512 * chip + 256 * ((k + 1 - own) % 2), 256), 256)
+            ref[pl.ds(row0 + 256 * own, 256), pl.ds(col0 + 256 * r, 256)] = S[r, :, cols].T
+
+    def turn_first(r):
+        for g in range(4):
+            turn(g, r)
 
     def squares(q):
         rs_t[q].wait_recv()
@@ -294,18 +314,28 @@
         copy.wait_recv()
     sxy[0].wait_recv()
     mapped(0)
+    for copy in t_up, t_dn, t_up1, t_dn1, t_up2, t_dn2:
+        copy.wait_send()
+    turn_first(0)
     squares(0)
     squares(1)
     squares(2)
     b_up.wait_recv()
     sxy[1].wait_recv()
     mapped(3)
+    turn_first(3)
     a_dn.wait_recv()
     sxy[2].wait_recv()
     mapped(1)
     squares(3)
     sq[0] = col[...].T[0:8, :]
     sq_c = [send(sq.at[0], sq.at[dy * 2 + dx], dy=dy, dxl=dx) for dy, dx in TENSOR]
+    turn_first(1)
+    a_up2.wait_recv()
+    b_dn2.wait_recv()
+    sxy[3].wait_recv()
+    mapped(2)
+    turn_first(2)
     for copy in sq_c:
         copy.wait_recv()
     total = sq[0]
@@ -332,13 +362,8 @@
         return acc
 
     acc = jnp.zeros((8, 128), F32)
-    for r in (0, 3, 1):
+    for r in range(4):
         acc = errors(r, acc)
-    a_up2.wait_recv()
-    b_dn2.wait_recv()
-    sxy[3].wait_recv()
-    mapped(2)
-    acc = errors(2, acc)
 
     row = lax.broadcasted_iota(jnp.int32, (8, 128), 0)
     tile = jnp.where(row == 0, jnp.max(amax_in), jnp.where(row == 1, jnp.max(amax_w), jnp.sum(acc)))
@@ -353,123 +378,180 @@
     scal[t] = tile
     sc1 = [send(scal.at[t], scal.at[t], dy=dy, dxl=dx) for dy, dx in TENSOR]
 
-    for copy in w_up, w_dn, w_up2, w_dn2, *w_sib:
+    for copy in w_up, w_dn, w_up2, w_dn2, *w_sib, *rs_t:
         copy.wait_send()
 
-    ORDER = [(1, 2), (0, 2), (1, 1), (0, 1), (1, 3), (0, 3), (1, 0), (0, 0)]
     a_cols, b_cols = pl.ds(0, ACOLS), pl.ds(ACOLS, 1024 - ACOLS)
 
-    def gslot(dxh, dz, cols):
+    def gslot(dxh, dz, cols, first=0, count=256):
         g = ORDER.index((dxh, dz))
-        return W.at[g // 2, pl.ds(256 * (g % 2), 256), cols]
-
-    to_sib, a_1, b_1, a_2 = [], {}, {}, {}
+        return W.at[g // 2, pl.ds(256 * (g % 2) + first, count), cols]
+
+    to_sib, a_1, b_1, a_2, a_m, b_m = [], {}, {}, {}, {}, {}
 
     def term(g):
         dxh, dz = ORDER[g]
-        chip = ((xh + dxh) % 2) * 4 + (z + dz) % 4
-        for other in (1, 0):
-            cols = pl.ds(pl.multiple_of(512 * chip + 256 * ((k + other) % 2), 256), 256)
-            st[pl.ds(256 * (1 - other), 256), :] = S[:, :, cols].reshape(1024, 256).T
-
-        @pl.loop(0, 4)
+        ref, row0, col0 = turned(g)
+
+        @pl.loop(0, 2)
         def _(n):
-            at = pl.multiple_of(256 * n, 256)
-            both = jnp.dot(st[...], E[:, pl.ds(at, 256)], preferred_element_type=F32).astype(BF16)
+            at = pl.multiple_of(512 * n, 512)
+            both = jnp.dot(
+                ref[pl.ds(row0, 512), pl.ds(col0, 1024)],
+                E[:, pl.ds(at, 512)],
+                preferred_element_type=F32,
+            ).astype(BF16)
             rows = pl.ds(256 * (g % 2), 256)
-            W[g // 2, rows, pl.ds(pl.multiple_of(1024 + at, 256), 256)] = both[:256]
-            W[g // 2, rows, pl.ds(at, 256)] = both[256:]
+            W[g // 2, rows, pl.ds(pl.multiple_of(1024 + at, 512), 512)] = both[:256]
+            W[g // 2, rows, pl.ds(at, 512)] = both[256:]
 
         to_sib.append(send(gslot(dxh, dz, pl.ds(1024, 1024)), sib.at[g], dk=1))
 
-    def add(dxh, dz, start, count, others):
+    def add(dxh, dz, cols, others, first=0, count=256):
         g = ORDER.index((dxh, dz))
 
-        @pl.loop(0, 16)
+        @pl.loop(0, count // 16)
         def _(i):
             here = pl.ds(pl.multiple_of(16 * i, 16), 16)
-            rows = pl.ds(pl.multiple_of(256 * (g % 2) + 16 * i, 16), 16)
-            cols = pl.ds(start, count)
+            there = pl.ds(pl.multiple_of(first + 16 * i, 16), 16)
+            rows = pl.ds(pl.multiple_of(256 * (g % 2) + first + 16 * i, 16), 16)
             total = W[g // 2, rows, cols].astype(F32)
-            for ref, index in others:
-                total = total + ref[index, here, :].astype(F32)
+            for ref, index, whole in others:
+                total = total + ref[index, there if whole else here, :].astype(F32)
             W[g // 2, rows, cols] = total.astype(BF16)
+
+    def along_z(dxh, dz, cols, mid, at, far, sent, passed):
+        if dz == 2:
+            passed[dxh, UP] = send(gslot(dxh, 2, cols, 0, 128), mid.at[at], dz=UP)
+            passed[dxh, DOWN] = send(gslot(dxh, 2, cols, 128, 128), mid.at[at + 1], dz=DOWN)
+        elif dz:
+            passed[dxh, dz].wait_recv()
+            add(dxh, dz, cols, [(mid, at + dz // 2, False)], 64 * (dz - 1), 128)
+            sent[dxh, dz] = send(gslot(dxh, dz, cols), far.at[at + dz // 2], dz=dz)
 
     def finish(g):
         dxh, dz = ORDER[g]
         to_sib[g].wait_recv()
-        add(dxh, dz, 0, 1024, [(sib, g)])
+        add(dxh, dz, pl.ds(0, 1024), [(sib, g, True)])
         if dxh:
             a_1[dz] = send(gslot(dxh, dz, a_cols), ra1.at[dz], dxh=1)
-        if dz:
-            b_1[dxh, dz] = send(gslot(dxh, dz, b_cols), rb1.at[dxh * 3 + dz - 1], dz=dz)
+
+    def second_b(dxh, dz):
+        along_z(dxh, dz, b_cols, bm, 2 * dxh, rb1, b_1, b_m)
 
     def second_a(dz):
         a_1[dz].wait_recv()
-        add(0, dz, 0, ACOLS, [(ra1, dz)])
-        if dz:
-            a_2[dz] = send(gslot(0, dz, a_cols), ra2.at[dz - 1], dz=dz)
-
-    for g in range(8):
+        add(0, dz, a_cols, [(ra1, dz, True)])
+        along_z(0, dz, a_cols, am, 0, ra2, a_2, a_m)
+
+    def term_of(g):
+        if g >= 4:
+            for r in range(4):
+                turn(g, r)
         term(g)
-        if g == 1:
-            for copy in sc1:
-                copy.wait_recv()
-            at = 8 + xh * 4 + z
-            scal[at] = merge(0, 8)
-            sc2 = [send(scal.at[at], scal.at[at], dxh=dx, dz=dz) for dx, dz in CONTEXT]
-        if g:
-            finish(g - 1)
-        if g == 4:
-            second_a(2)
-        if g == 6:
-            second_a(1)
-    finish(7)
+
+    term_of(0)
+    term_of(1)
+    for copy in sc1:
+        copy.wait_recv()
+    at = 8 + xh * 4 + z
+    scal[at] = merge(0, 8)
+    sc2 = [send(scal.at[at], scal.at[at], dxh=dx, dz=dz) for dx, dz in CONTEXT]
+    finish(0)
+    second_b(1, 2)
+    term_of(2)
+    finish(1)
+    second_b(0, 2)
+    term_of(3)
+    finish(2)
+    second_b(1, 1)
+    term_of(4)
+    finish(3)
+    second_b(1, 3)
+    second_a(2)
+    term_of(5)
+    finish(4)
+    term_of(6)
+    finish(5)
+    second_b(0, 1)
+    term_of(7)
+    finish(6)
+    second_b(0, 3)
+    for n in (UP, DOWN):
+        b_1[1, n].wait_recv()
+    add(1, 0, b_cols, [(rb1, 2, True), (rb1, 3, True)])
+    b_2 = send(gslot(1, 0, b_cols), rb2.at[0], dxh=1)
+    second_a(1)
     second_a(3)
-
     for copy in sc2:
         copy.wait_recv()
     scal[16 + k] = merge(8, 8)
     sc3 = send(scal.at[16 + k], scal.at[16 + k], dk=1)
-
-    for dz in (1, 2, 3):
-        b_1[1, dz].wait_recv()
-    add(1, 0, ACOLS, 1024 - ACOLS, [(rb1, 3), (rb1, 4), (rb1, 5)])
-    b_2 = send(gslot(1, 0, b_cols), rb2.at[0], dxh=1)
+    finish(7)
     second_a(0)
-
-    for dz in (1, 2, 3):
-        b_1[0, dz].wait_recv()
-        a_2[dz].wait_recv()
+    sc3.wait_recv()
+    scal[18] = merge(16, 2)
+    written = [load(scal.at[18], parts.at[pl.ds(256, 8), pl.ds(0, 128)])]
+
+    for n in (UP, DOWN):
+        b_1[0, n].wait_recv()
+        a_2[0, n].wait_recv()
     b_2.wait_recv()
     scale = 1.0 / math.sqrt(tokens_all)
-
-    @pl.loop(0, 16)
-    def _(i):
-        rows = pl.ds(pl.multiple_of(16 * i, 16), 16)
-        mine = pl.ds(pl.multiple_of(256 + 16 * i, 16), 16)
-        total = W[3, mine, a_cols].astype(F32)
-        for n in range(3):
-            total = total + ra2[n, rows, :].astype(F32)
-        grad[rows, a_cols] = total * scale
-        total = W[3, mine, b_cols].astype(F32) + rb2[0, rows, :].astype(F32)
-        for n in range(3):
-            total = total + rb1[n, rows, :].astype(F32)
-        grad[rows, b_cols] = total * scale
-
-    sc3.wait_recv()
-    final = merge(16, 2)
-    hist_in_new[0] = jnp.max(jnp.where(row == 0, final, 0.0))
-    hist_w_new[0] = jnp.max(jnp.where(row == 1, final, 0.0))
-    loss[0] = jnp.max(jnp.where(row == 2, final, 0.0)) * (0.5 / (tokens_all * 8192))
+    for q in range(2):
+
+        @pl.loop(0, 8)
+        def _(i):
+            rows = pl.ds(pl.multiple_of(128 * q + 16 * i, 16), 16)
+            mine = pl.ds(pl.multiple_of(256 + 128 * q + 16 * i, 16), 16)
+            total = W[3, mine, a_cols].astype(F32)
+            for n in range(2):
+                total = total + ra2[n, rows, :].astype(F32)
+            total_g[rows, a_cols] = total * scale
+            total = W[3, mine, b_cols].astype(F32) + rb2[0, rows, :].astype(F32)
+            for n in range(2):
+                total = total + rb1[n, rows, :].astype(F32)
+            total_g[rows, b_cols] = total * scale
+
+        rows = pl.ds(128 * q, 128)
+        written.append(load(total_g.at[rows], parts.at[rows]))
+
+    waited = [w_up, w_dn, w_up2, w_dn2, *w_sib, t_up, t_dn, t_up1, t_dn1, t_up2, t_dn2, *rs_t]
+    for copy in sends:
+        if not any(copy is w for w in waited):
+            copy.wait_send()
+    for copy in written:
+        copy.wait()
+
+
+def results(
+    tokens_all, parts, hist_in, hist_w, grad, loss, hist_in_new, hist_w_new, held, tile, sem_in, sem_out
+):
+    scalars = pltpu.make_async_copy(parts.at[pl.ds(256, 8), pl.ds(0, 128)], tile, sem_in.at[4])
+    scalars.start()
+    pieces = [pl.ds(64 * i, 64) for i in range(4)]
+    ins = [
+        pltpu.make_async_copy(parts.at[rows], held.at[rows], sem_in.at[i])
+        for i, rows in enumerate(pieces)
+    ]
+    outs = [
+        pltpu.make_async_copy(held.at[rows], grad.at[rows], sem_out.at[i])
+        for i, rows in enumerate(pieces)
+    ]
+    for copy in ins:
+        copy.start()
     for i in range(15):
         hist_in_new[i + 1] = hist_in[i]
         hist_w_new[i + 1] = hist_w[i]
-
-    waited = [w_up, w_dn, w_up2, w_dn2, *w_sib]
-    for copy in sends:
-        if not any(copy is w for w in waited):
-            copy.wait_send()
+    for copy, back in zip(ins, outs):
+        copy.wait()
+        back.start()
+    scalars.wait()
+    hist_in_new[0] = jnp.max(tile[0:1, :])
+    hist_w_new[0] = jnp.max(tile[1:2, :])
+    loss[0] = jnp.max(tile[2:3, :]) * (0.5 / (tokens_all * 8192))
+    for back in outs:
+        back.wait()
 
 
 def local(
@@ -480,17 +562,12 @@
     smem = pl.BlockSpec(memory_space=pltpu.SMEM)
     vmem = pl.BlockSpec(memory_space=pltpu.VMEM)
     hbm = pl.BlockSpec(memory_space=pl.ANY)
-    grad, hist_in, hist_w, loss = pl.pallas_call(
+    parts = pl.pallas_call(
         functools.partial(kernel, tokens_all),
         name="distill",
-        out_shape=(
-            jax.ShapeDtypeStruct((256, 1024), F32),
-            jax.ShapeDtypeStruct((16,), F32),
-            jax.ShapeDtypeStruct((16,), F32),
-            jax.ShapeDtypeStruct((1,), F32),
-        ),
+        out_shape=jax.ShapeDtypeStruct((264, 1024), F32),
         in_specs=[smem, smem, vmem, vmem, hbm, hbm, hbm, hbm, hbm],
-        out_specs=(vmem, smem, smem, smem),
+        out_specs=hbm,
         scratch_shapes=[
             pltpu.VMEM((1024, 2048), BF16),
             pltpu.VMEM((4, 512, 2048), BF16),
@@ -506,16 +583,18 @@
             pltpu.VMEM((64, 8192), BF16),
             pltpu.VMEM((1024, 128), F32),
             pltpu.VMEM((8, 8, 1024), F32),
-            pltpu.VMEM((18, 8, 128), F32),
+            pltpu.VMEM((19, 8, 128), F32),
             pltpu.VMEM((8, 256, 1024), BF16),
             pltpu.VMEM((4, 256, ACOLS), BF16),
-            pltpu.VMEM((3, 256, ACOLS), BF16),
-            pltpu.VMEM((6, 256, 1024 - ACOLS), BF16),
+            pltpu.VMEM((2, 256, ACOLS), BF16),
+            pltpu.VMEM((4, 256, 1024 - ACOLS), BF16),
             pltpu.VMEM((1, 256, 1024 - ACOLS), BF16),
-            pltpu.VMEM((512, 1024), BF16),
+            pltpu.VMEM((2, 128, ACOLS), BF16),
+            pltpu.VMEM((4, 128, 1024 - ACOLS), BF16),
+            pltpu.VMEM((256, 1024), F32),
             pltpu.SemaphoreType.DMA((COPIES,)),
             pltpu.SemaphoreType.DMA((COPIES,)),
-            pltpu.SemaphoreType.DMA((6,)),
+            pltpu.SemaphoreType.DMA((10,)),
         ],
         compiler_params=pltpu.CompilerParams(
             collective_id=0, has_side_effects=True, vmem_limit_bytes=62 << 20
@@ -534,6 +613,24 @@
         student_hidden,
         projection,
     )
+    grad, loss, hist_in, hist_w = pl.pallas_call(
+        functools.partial(results, tokens_all),
+        name="results",
+        out_shape=(
+            jax.ShapeDtypeStruct((256, 1024), F32),
+            jax.ShapeDtypeStruct((1,), F32),
+            jax.ShapeDtypeStruct((16,), F32),
+            jax.ShapeDtypeStruct((16,), F32),
+        ),
+        in_specs=[hbm, smem, smem],
+        out_specs=(hbm, smem, smem, smem),
+        scratch_shapes=[
+            pltpu.VMEM((256, 1024), F32),
+            pltpu.VMEM((8, 128), F32),
+            pltpu.SemaphoreType.DMA((5,)),
+            pltpu.SemaphoreType.DMA((4,)),
+        ],
+    )(parts, input_history, weight_history)
     return grad, loss.reshape(()), hist_in, hist_w
 
 

time: 172 us -> 161 us (0.936)
  Pallas kernels: 165 us -> 160 us
  local copies, waits for them, and re-layouts: 4.56 us -> 0 us
  between operations: 2.41 us -> 0.64 us
    pallas_call x1, Pallas kernels: 165 us -> 157 us  [local(): pl.pallas_call(functools.partial(kernel, tokens_all), name='distill', out...]
    unnamed x3 -> x0, local copies, waits for them, and re-layouts: 4.56 us -> none
    pallas_call x0 -> x1, Pallas kernels: none -> 3.2 us  [local(): pl.pallas_call(functools.partial(results, tokens_all), name='results', ou...]
where the time goes in v3:
time: 161 us
  Pallas kernels  160 us (99%)
    pallas_call x1, Pallas kernels, local(): pl.pallas_call(functools.partial(kernel, tokens_all), name='distill', out...  157 us

profile of v3, /device:TPU:0, one launch (start us, length us, event | category | flops | bytes accessed | tf_op | source)
XLA Modules:
  0.0 161.0 jit_solution(17891578283515807092)
XLA Ops:
  0.6 157.1 %distill.1.parts = f32[264,1024]{1,0:T(8,128)} custom-call(f32[16]{0:T(128)} %hist_in.3, f32[16]{0:T(128)} %hist_w.3, f32[1,4096]{1,0:T(1,128)} %bitcast.4, f32[1,8192]{1,0:T(1,128)} %bitcast.3, bf16[1024,512]{1,0:T(8,128)(2,1)} %tin.1, bf16[1024,1024]{1,0:T(8,128)(2,1)} %resid.1, bf16[512,8192]{1,0:T(8,128)(2,1)} %wo.1, bf16[128,4096]{1,0:T(8,128)(2,1)} %stu.1, ...), custom_call_target="tpu_custom_call" | custom-call | flops 25769803776 | bytes 16777216 | tf_op jit(solution)/shard_map/distill/pallas_call | solution.py:565
  157.8 3.2 %results.1 = (f32[256,1024]{1,0:T(8,128)}, f32[1]{0:T(128)}, f32[16]{0:T(128)}, f32[16]{0:T(128)}) custom-call(f32[264,1024]{1,0:T(8,128)} %distill.1.parts, f32[16]{0:T(128)} %hist_in.3, f32[16]{0:T(128)} %hist_w.3), custom_call_target="tpu_custom_call" | custom-call | tf_op jit(solution)/shard_map/results/pallas_call | solution.py:616

commit v4 on v3

--- a/solution.py
+++ b/solution.py
@@ -11,8 +11,9 @@
 MESH = pl.DeviceIdType.MESH
 F32, BF16 = jnp.float32, jnp.bfloat16
 EPS = 1e-05
-COPIES = 100
-XROWS = 96
+SEND_SEMS, RECV_SEMS = 7, 84
+GROUP = 8 << 20
+XROWS = 112
 ACOLS = 384
 
 
@@ -38,7 +39,7 @@
     tokens_all,
     hist_in, hist_w, stu_gain, tea_gain, tin, resid, wo, stu, proj,
     parts,
-    T, W, S, PR, R, H, M, E, psend, precv, sraw, wraw, col, sq, scal, sib, ra1, ra2, rb1, rb2, am, bm, total_g,
+    T, W, S, PR, R, H, M, E, psend, precv, sraw, wraw, col, sq, scal, sib, ra1, ra2, rb1, rb2, am, bm, total_g, sgain, tgain,
     ssem, rsem, lsem,
 ):
     t, c = lax.axis_index("tensor"), lax.axis_index("context")
@@ -50,21 +51,58 @@
         nxl, nxh, nk = (xl + dxl) % 2, (xh + dxh) % 2, (k + dk) % 2
         return {"tensor": ny * 2 + nxl, "context": nxh * 8 + nz * 2 + nk}
 
-    sends = []
-
-    def send(src, dst, **to):
-        i = len(sends)
-        copy = pltpu.make_async_remote_copy(
+    received, groups = [], {}
+
+    def remote(src, dst, send_sem, recv_sem, to):
+        return pltpu.make_async_remote_copy(
             src_ref=src,
             dst_ref=dst,
-            send_sem=ssem.at[i],
-            recv_sem=rsem.at[i],
-            device_id=dev(**to),
+            send_sem=ssem.at[send_sem],
+            recv_sem=rsem.at[recv_sem],
+            device_id=to,
             device_id_type=MESH,
         )
+
+    def size(ref):
+        return math.prod(ref.shape) * jnp.dtype(ref.dtype).itemsize
+
+    def send(src, dst, group=None, **to):
+        if group is None:
+            group = next((n for n in range(50) if groups.get(n, (0, 0))[1] + size(src) <= GROUP), 0)
+        index, held = groups.get(group, (len(groups), 0))
+        groups[group] = index, held + size(src)
+        received.append(len(received))
+        copy = remote(src, dst, index, received[-1], dev(**to))
         copy.start()
-        sends.append(copy)
         return copy
+
+    def span(count):
+        if count % 32768 == 0:
+            return PR.at[pl.ds(0, count // 2048)]
+        return col.at[pl.ds(0, count // 512)]
+
+    def sent(group):
+        index, held = groups[group]
+        rows = span(held)
+        remote(rows, rows, index, 0, dev(dk=1)).wait_send()
+
+    def send_all(pieces, group=None):
+        received.append(len(received))
+        at, total = received[-1], 0
+        for src, dst, to in pieces:
+            key = group
+            if key is None:
+                key = next(n for n in range(50) if groups.get(n, (0, 0))[1] + size(src) <= GROUP)
+            index, held = groups.get(key, (len(groups), 0))
+            groups[key] = index, held + size(src)
+            remote(src, dst, index, at, dev(**to)).start()
+            total += size(src)
+        return at, total
+
+    def await_group(landed):
+        at, total = landed
+        rows = span(total)
+        remote(rows, rows, 0, at, dev(dk=1)).wait_recv()
 
     local = []
 
@@ -78,10 +116,12 @@
     CONTEXT = [(dx, dz) for dx in range(2) for dz in range(4) if (dx, dz) != (0, 0)]
     UP, DOWN = 1, 3
 
-    slab = pl.multiple_of(64 * (2 * z + k), 64)
-    l_wraw = load(wo.at[pl.ds(slab, 64)], wraw)
+    slab = pl.multiple_of(64 * (2 * z + k) + 32 * xh, 32)
+    l_wraw = load(wo.at[pl.ds(slab, 32)], wraw)
+    l_sgain = load(stu_gain, sgain)
+    l_tgain = load(tea_gain.at[:, pl.ds(pl.multiple_of(1024 * t, 1024), 1024)], tgain)
+    l_proj = load(proj, PR.at[pl.ds(pl.multiple_of(256 * c, 256), 256)])
     l_stu = load(stu, sraw)
-    l_proj = load(proj, PR.at[pl.ds(pl.multiple_of(256 * c, 256), 256)])
     l_tin = load(tin, T.at[:, pl.ds(0, 512)])
     l_wown = load(wo.at[:, pl.ds(pl.multiple_of(2048 * y, 2048), 2048)], W.at[0])
     l_res = load(resid, R)
@@ -109,18 +149,35 @@
             wraw[rows, cols] = jnp.clip(v, -lim_w, lim_w).astype(BF16)
         return amax
 
-    amax_w = lax.fori_loop(0, 4, clip_w, jnp.zeros((8, 128), F32))
+    amax_w = lax.fori_loop(0, 2, clip_w, jnp.zeros((8, 128), F32))
+
+    pl.semaphore_wait(barrier, len(TENSOR) + len(CONTEXT) + 1)
+
+    def wcols(d):
+        return pl.ds(pl.multiple_of(2048 * ((y + d) % 4), 2048), 2048)
+
+    w_y = send_all(
+        [(wraw.at[:, wcols(d)], W.at[4 - d, pl.ds(slab, 32)], {"dy": d}) for d in (2, 1, 3)]
+    )
+    l_proj.wait()
+
+    def pblock(dxh=0, dz=0):
+        at = ((xh + dxh) % 2) * 8 + ((z + dz) % 4) * 2 + k
+        return PR.at[pl.ds(pl.multiple_of(256 * at, 256), 256)]
+
+    p_up = send(pblock(), pblock(), dz=UP)
+    p_dn = send(pblock(), pblock(), dz=DOWN)
+    p_sib = [send(pblock(), pblock(), dk=1)]
 
     l_stu.wait()
+    l_sgain.wait()
 
     @pl.loop(0, 8)
     def _(i):
         rows = pl.ds(pl.multiple_of(16 * i, 16), 16)
         v = sraw[rows, :].astype(F32)
         mean = jnp.mean(v * v, axis=1, keepdims=True)
-        S[0, rows, :] = (v * lax.rsqrt(mean + EPS) * stu_gain[...]).astype(BF16)
-
-    pl.semaphore_wait(barrier, len(TENSOR) + len(CONTEXT) + 1)
+        S[0, rows, :] = (v * lax.rsqrt(mean + EPS) * sgain[...]).astype(BF16)
 
     nx = XROWS
     ny = 128 - nx
@@ -128,24 +185,6 @@
     far_x, far_y = pl.ds(128, nx), pl.ds(128 + nx, ny)
     sy_up = send(S.at[0, own_y], S.at[3, own_y], dy=UP)
     sy_dn = send(S.at[0, own_y], S.at[1, own_y], dy=DOWN)
-
-    def wcols(d):
-        return pl.ds(pl.multiple_of(2048 * ((y + d) % 4), 2048), 2048)
-
-    w_y = [
-        send(wraw.at[:, wcols(d)], W.at[4 - d, pl.ds(slab, 64)], dy=d) for d in (2, 1, 3)
-    ]
-    l_proj.wait()
-
-    def pblock(dxh=0, dz=0):
-        at = ((xh + dxh) % 2) * 8 + ((z + dz) % 4) * 2 + k
-        return PR.at[pl.ds(pl.multiple_of(256 * at, 256), 256)]
-
-    p_x = send(pblock(), pblock(), dxh=1)
-    p_up = send(pblock(), pblock(), dz=UP)
-    p_dn = send(pblock(), pblock(), dz=DOWN)
-    p_sib = [send(pblock(), pblock(), dk=1)]
-    sx = send(S.at[0, own_x], S.at[0, far_x], dxl=1)
     sxy = [send(S.at[0, own_y], S.at[0, far_y], dxl=1)]
 
     l_tin.wait()
@@ -157,39 +196,28 @@
         return jnp.maximum(amax, fold(jnp.maximum, jnp.abs(v)))
 
     amax_in = lax.fori_loop(0, 32, clip_t, jnp.zeros((8, 128), F32))
-
     low, high = pl.ds(0, 512), pl.ds(512, 512)
 
     def tblock(r, rows):
         return T.at[rows, pl.ds(512 * r, 512)]
 
-    t_up = send(tblock(0, low), tblock(3, low), dy=UP)
-    t_dn = send(tblock(0, high), tblock(1, high), dy=DOWN)
-
-    left, right = pl.ds(0, 2048), pl.ds(2048, 2048)
-    sy_up.wait_recv()
-    sy_up2 = send(S.at[3, own_y, left], S.at[2, own_y, left], dy=UP)
-    sxy.append(send(S.at[3, own_y], S.at[3, far_y], dxl=1))
-    sy_dn.wait_recv()
-    sy_dn2 = send(S.at[1, own_y, right], S.at[2, own_y, right], dy=DOWN)
-    sxy.append(send(S.at[1, own_y], S.at[1, far_y], dxl=1))
-
-    t_up1 = send(tblock(0, high), tblock(3, high), dy=UP)
-    t_dn1 = send(tblock(0, low), tblock(1, low), dy=DOWN)
-
-    def wslab(dz=0, half=None):
+    t_up = send(tblock(0, low), tblock(3, low), "t", dy=UP)
+    t_dn = send(tblock(0, high), tblock(1, high), "t", dy=DOWN)
+    t_up1 = send(tblock(0, high), tblock(3, high), "t", dy=UP)
+    t_dn1 = send(tblock(0, low), tblock(1, low), "t", dy=DOWN)
+
+    def wslab(dz=0, dxh=None):
         at = pl.multiple_of(64 * (2 * ((z + dz) % 4) + k), 64)
-        if half is None:
+        if dxh is None:
             return W.at[pl.ds(1, 3), pl.ds(at, 64)]
-        return W.at[pl.ds(1, 3), pl.ds(pl.multiple_of(at + 32 * half, 32), 32)]
-
-    p_x.wait_recv()
-    p_sib.append(send(pblock(1), pblock(1), dk=1))
-    for copy in w_y:
-        copy.wait_recv()
-    w_up = send(wslab(), wslab(), dz=UP)
-    w_dn = send(wslab(), wslab(), dz=DOWN)
-    w_sib = [send(wslab(), wslab(), dk=1)]
+        return W.at[pl.ds(1, 3), pl.ds(pl.multiple_of(at + 32 * ((xh + dxh) % 2), 32), 32)]
+
+    await_group(w_y)
+    w_x = send(wslab(0, 0), wslab(0, 0), "w", dxh=1)
+    w_up = send(wslab(0, 0), wslab(0, 0), "w", dz=UP)
+    w_dn = send(wslab(0, 0), wslab(0, 0), "w", dz=DOWN)
+    sx = send(S.at[0, own_x], S.at[0, far_x], dxl=1)
+    p_x = send(pblock(), pblock(), dxh=1)
 
     l_wown.wait()
 
@@ -199,36 +227,46 @@
         v = W[0, rows, :].astype(F32)
         W[0, rows, :] = jnp.clip(v, -lim_w, lim_w).astype(BF16)
 
-    sy_up2.wait_recv()
-    sy_dn2.wait_recv()
-    sxy.append(send(S.at[2, own_y], S.at[2, far_y], dxl=1))
-
+    sy_up.wait_recv()
+    sxy.append(send(S.at[3, own_y], S.at[3, far_y], dxl=1))
+    sy_dn.wait_recv()
+    sxy.append(send(S.at[1, own_y], S.at[1, far_y], dxl=1))
+    w_x.wait_recv()
+    v_dn = send(wslab(0, 1), wslab(0, 1), "w", dz=DOWN)
+    v_up = send(wslab(0, 1), wslab(0, 1), "w", dz=UP)
+    w_sib = [send(wslab(), wslab(), "w", dk=1)]
+
+    left, right = pl.ds(0, 2048), pl.ds(2048, 2048)
     t_up.wait_recv()
-    t_up2 = send(tblock(3, low), tblock(2, low), dy=UP)
+    t_up2 = send(tblock(3, low), tblock(2, low), "t", dy=UP)
     t_dn.wait_recv()
-    t_dn2 = send(tblock(1, high), tblock(2, high), dy=DOWN)
+    t_dn2 = send(tblock(1, high), tblock(2, high), "t", dy=DOWN)
+    sy_up2 = send(S.at[3, own_y, left], S.at[2, own_y, left], dy=UP)
+    sy_dn2 = send(S.at[1, own_y, right], S.at[2, own_y, right], dy=DOWN)
     a_up = send(S.at[0, own_x], S.at[3, own_x], dy=UP)
+
+    w_up.wait_recv()
+    w_up2 = send(wslab(DOWN, 0), wslab(DOWN, 0), "w", dz=UP)
+    v_dn.wait_recv()
+    v_dn2 = send(wslab(UP, 1), wslab(UP, 1), "w", dz=DOWN)
+    v_up.wait_recv()
+    w_sib.append(send(wslab(DOWN), wslab(DOWN), "w", dk=1))
+    w_dn.wait_recv()
+    w_sib.append(send(wslab(UP), wslab(UP), "w", dk=1))
+
     sx.wait_recv()
     b_dn = send(S.at[0, far_x], S.at[1, far_x], dy=DOWN)
     b_up = send(S.at[0, far_x], S.at[3, far_x], dy=UP)
     a_dn = send(S.at[0, own_x], S.at[1, own_x], dy=DOWN)
 
-    w_up.wait_recv()
-    w_up2 = send(wslab(DOWN, 0), wslab(DOWN, 0), dz=UP)
-    w_sib.append(send(wslab(DOWN), wslab(DOWN), dk=1))
-    w_dn.wait_recv()
-    w_dn2 = send(wslab(UP, 1), wslab(UP, 1), dz=DOWN)
-    w_sib.append(send(wslab(UP), wslab(UP), dk=1))
-    q_dn = send(pblock(1), pblock(1), dz=DOWN)
-    q_up = send(pblock(1), pblock(1), dz=UP)
+    w_up2.wait_recv()
+    v_dn2.wait_recv()
+    w_sib.append(send(wslab(2), wslab(2), "w", dk=1))
     p_up.wait_recv()
     p_up2 = send(pblock(0, DOWN), pblock(0, DOWN), dz=UP)
     p_sib.append(send(pblock(0, DOWN), pblock(0, DOWN), dk=1))
     p_dn.wait_recv()
     p_sib.append(send(pblock(0, UP), pblock(0, UP), dk=1))
-    w_up2.wait_recv()
-    w_dn2.wait_recv()
-    w_sib.append(send(wslab(2), wslab(2), dk=1))
 
     for copy in t_up1, t_dn1, t_up2, t_dn2, *w_sib:
         copy.wait_recv()
@@ -247,14 +285,18 @@
             cols = pl.ds(pl.multiple_of(256 * n, 256), 256)
             psend[rows, cols] = product(rows, 1024 * (1 - xl), n).astype(BF16)
 
-        rs_t.append(send(psend.at[rows], precv.at[rows], dxl=1))
-        if q == 1:
-            q_dn.wait_recv()
-            q_dn2 = send(pblock(1, UP), pblock(1, UP), dz=DOWN)
-            p_sib.append(send(pblock(1, UP), pblock(1, UP), dk=1))
-            q_up.wait_recv()
-            p_sib.append(send(pblock(1, DOWN), pblock(1, DOWN), dk=1))
-
+        for rows in (rows,) if q < 3 else (pl.ds(768, 128), pl.ds(896, 128)):
+            rs_t.append(send(psend.at[rows], precv.at[rows], "r", dxl=1))
+        if q == 0:
+            p_x.wait_recv()
+            p_sib.append(send(pblock(1), pblock(1), dk=1))
+            q_dn = send(pblock(1), pblock(1), dz=DOWN)
+            q_up = send(pblock(1), pblock(1), dz=UP)
+
+
+    sy_up2.wait_recv()
+    sy_dn2.wait_recv()
+    sxy.append(send(S.at[2, own_y], S.at[2, far_y], dxl=1))
     l_res.wait()
     for q in range(4):
         rows = pl.ds(256 * q, 256)
@@ -264,14 +306,20 @@
             cols = pl.ds(pl.multiple_of(256 * n, 256), 256)
             H[rows, cols] = product(rows, 1024 * xl, n) + R[rows, cols].astype(F32)
 
+    q_dn.wait_recv()
+    q_dn2 = send(pblock(1, UP), pblock(1, UP), dz=DOWN)
+    p_sib.append(send(pblock(1, UP), pblock(1, UP), dk=1))
+    q_up.wait_recv()
+    p_sib.append(send(pblock(1, DOWN), pblock(1, DOWN), dk=1))
     p_up2.wait_recv()
     p_sib.append(send(pblock(0, 2), pblock(0, 2), dk=1))
+    parts_x = [(pl.ds(0, 64), pl.ds(64, nx - 64)), (pl.ds(128, 64), pl.ds(192, nx - 64))]
+    a_up.wait_recv()
+    a_up2, a_up3 = [send(S.at[3, rows], S.at[2, rows], dy=UP) for rows in parts_x[0]]
+    b_dn.wait_recv()
+    b_dn2, b_dn3 = [send(S.at[1, rows], S.at[2, rows], dy=DOWN) for rows in parts_x[1]]
     q_dn2.wait_recv()
     p_sib.append(send(pblock(1, 2), pblock(1, 2), dk=1))
-    a_up.wait_recv()
-    a_up2 = send(S.at[3, own_x], S.at[2, own_x], dy=UP)
-    b_dn.wait_recv()
-    b_dn2 = send(S.at[1, far_x], S.at[2, far_x], dy=DOWN)
 
     def mapped(r):
         @pl.loop(0, 2)
@@ -281,6 +329,15 @@
                 S[r], PR[:, cols], preferred_element_type=F32
             )
 
+    def mapped_part(first):
+        @pl.loop(0, 2)
+        def _(n):
+            cols = pl.ds(pl.multiple_of(512 * n, 512), 512)
+            rows = jnp.concatenate([S[2, pl.ds(first, 64)], S[2, pl.ds(128 + first, 64)]], axis=0)
+            out = jnp.dot(rows, PR[:, cols], preferred_element_type=F32)
+            M[pl.ds(512 + first, 64), cols] = out[:64]
+            M[pl.ds(640 + first, 64), cols] = out[64:]
+
     ORDER = [(1, 2), (0, 2), (1, 1), (1, 3), (1, 0), (0, 1), (0, 3), (0, 0)]
 
     def turned(g):
@@ -300,22 +357,25 @@
         for g in range(4):
             turn(g, r)
 
+    l_tgain.wait()
+    gains = tgain[...]
+
     def squares(q):
         rs_t[q].wait_recv()
-
-        @pl.loop(0, 16)
+        first, count = (256 * q, 256) if q < 3 else (128 * q + 384, 128)
+
+        @pl.loop(0, count // 16)
         def _(i):
-            rows = pl.ds(pl.multiple_of(256 * q + 16 * i, 16), 16)
+            rows = pl.ds(pl.multiple_of(first + 16 * i, 16), 16)
             h = H[rows, :] + precv[rows, :].astype(F32)
-            H[rows, :] = h
+            H[rows, :] = h * gains
             col[rows, :] = jnp.broadcast_to(jnp.sum(h * h, axis=1, keepdims=True), (16, 128))
 
     for copy in p_sib:
         copy.wait_recv()
     sxy[0].wait_recv()
     mapped(0)
-    for copy in t_up, t_dn, t_up1, t_dn1, t_up2, t_dn2:
-        copy.wait_send()
+    sent("t")
     turn_first(0)
     squares(0)
     squares(1)
@@ -328,44 +388,50 @@
     sxy[2].wait_recv()
     mapped(1)
     squares(3)
-    sq[0] = col[...].T[0:8, :]
-    sq_c = [send(sq.at[0], sq.at[dy * 2 + dx], dy=dy, dxl=dx) for dy, dx in TENSOR]
+    squares(4)
+    row = lax.broadcasted_iota(jnp.int32, (8, 128), 0)
+    packed = jnp.zeros((8, 128), F32)
+    for i in range(8):
+        packed = jnp.where(row == i, col[pl.ds(128 * i, 128), :].T[0:8, :], packed)
+    sq[0] = packed
+    sq_c = send_all(
+        [(sq.at[0], sq.at[dy * 2 + dx], {"dy": dy, "dxl": dx}) for dy, dx in TENSOR], "s"
+    )
     turn_first(1)
+
+    def errors(r, acc):
+        for b in range(2):
+            base = 128 * (2 * ((y + r) % 4) + (xl + b) % 2)
+
+            def step(i, acc):
+                there = pl.ds(pl.multiple_of(base + 16 * i, 16), 16)
+                here = pl.ds(pl.multiple_of(256 * r + 128 * b + 16 * i, 16), 16)
+                scale = jnp.concatenate([col[there, :]] * 8, axis=1)
+                e = M[here, :] - H[there, :] * scale
+                E[here, :] = e.astype(BF16)
+                return acc + fold(jnp.add, e * e)
+
+            acc = lax.fori_loop(0, 8, step, acc)
+        return acc
+
     a_up2.wait_recv()
     b_dn2.wait_recv()
+    mapped_part(0)
     sxy[3].wait_recv()
-    mapped(2)
-    turn_first(2)
-    for copy in sq_c:
-        copy.wait_recv()
+    a_up3.wait_recv()
+    b_dn3.wait_recv()
+    mapped_part(64)
+    await_group(sq_c)
     total = sq[0]
     for i in range(1, 8):
         total = total + sq[i]
     inv = lax.rsqrt(total * (1.0 / 8192) + EPS)
-    col[...] = jnp.broadcast_to(inv[0:1, :], (128, 1024)).T
-
-    gains = tea_gain[:, pl.ds(pl.multiple_of(1024 * t, 1024), 1024)]
-
-    def errors(r, acc):
-        for b in range(2):
-            base = 128 * (2 * ((y + r) % 4) + (xl + b) % 2)
-
-            def step(i, acc):
-                there = pl.ds(pl.multiple_of(base + 16 * i, 16), 16)
-                here = pl.ds(pl.multiple_of(256 * r + 128 * b + 16 * i, 16), 16)
-                scale = jnp.concatenate([col[there, :]] * 8, axis=1)
-                e = M[here, :] - H[there, :] * scale * gains
-                E[here, :] = e.astype(BF16)
-                return acc + fold(jnp.add, e * e)
-
-            acc = lax.fori_loop(0, 8, step, acc)
-        return acc
-
+    for i in range(8):
+        col[pl.ds(128 * i, 128), :] = jnp.broadcast_to(inv[i : i + 1, :], (128, 128)).T
     acc = jnp.zeros((8, 128), F32)
     for r in range(4):
         acc = errors(r, acc)
 
-    row = lax.broadcasted_iota(jnp.int32, (8, 128), 0)
     tile = jnp.where(row == 0, jnp.max(amax_in), jnp.where(row == 1, jnp.max(amax_w), jnp.sum(acc)))
 
     def merge(first, count):
@@ -376,10 +442,10 @@
         return out
 
     scal[t] = tile
-    sc1 = [send(scal.at[t], scal.at[t], dy=dy, dxl=dx) for dy, dx in TENSOR]
-
-    for copy in w_up, w_dn, w_up2, w_dn2, *w_sib, *rs_t:
-        copy.wait_send()
+    sc1 = send_all([(scal.at[t], scal.at[t], {"dy": dy, "dxl": dx}) for dy, dx in TENSOR], "s")
+
+    sent("w")
+    sent("r")
 
     a_cols, b_cols = pl.ds(0, ACOLS), pl.ds(ACOLS, 1024 - ACOLS)
 
@@ -392,6 +458,24 @@
     def term(g):
         dxh, dz = ORDER[g]
         ref, row0, col0 = turned(g)
+
+        if g == 0:
+            for own in (0, 1):
+
+                @pl.loop(0, 2)
+                def _(n):
+                    at = pl.multiple_of(512 * n, 512)
+                    one = jnp.dot(
+                        ref[pl.ds(row0 + 256 * own, 256), pl.ds(col0, 1024)],
+                        E[:, pl.ds(at, 512)],
+                        preferred_element_type=F32,
+                    )
+                    start = pl.multiple_of(1024 * (1 - own) + at, 512)
+                    W[0, pl.ds(0, 256), pl.ds(start, 512)] = one.astype(BF16)
+
+                if own == 0:
+                    to_sib.append(send(gslot(dxh, dz, pl.ds(1024, 1024)), sib.at[g], dk=1))
+            return
 
         @pl.loop(0, 2)
         def _(n):
@@ -445,20 +529,18 @@
         along_z(0, dz, a_cols, am, 0, ra2, a_2, a_m)
 
     def term_of(g):
-        if g >= 4:
-            for r in range(4):
-                turn(g, r)
+        for r in range(4) if g >= 4 else (2,):
+            turn(g, r)
         term(g)
 
     term_of(0)
     term_of(1)
-    for copy in sc1:
-        copy.wait_recv()
+    finish(0)
+    second_b(1, 2)
+    await_group(sc1)
     at = 8 + xh * 4 + z
     scal[at] = merge(0, 8)
-    sc2 = [send(scal.at[at], scal.at[at], dxh=dx, dz=dz) for dx, dz in CONTEXT]
-    finish(0)
-    second_b(1, 2)
+    sc2 = send_all([(scal.at[at], scal.at[at], {"dxh": dx, "dz": dz}) for dx, dz in CONTEXT], "s")
     term_of(2)
     finish(1)
     second_b(0, 2)
@@ -483,10 +565,9 @@
     b_2 = send(gslot(1, 0, b_cols), rb2.at[0], dxh=1)
     second_a(1)
     second_a(3)
-    for copy in sc2:
-        copy.wait_recv()
+    await_group(sc2)
     scal[16 + k] = merge(8, 8)
-    sc3 = send(scal.at[16 + k], scal.at[16 + k], dk=1)
+    sc3 = send(scal.at[16 + k], scal.at[16 + k], "s", dk=1)
     finish(7)
     second_a(0)
     sc3.wait_recv()
@@ -516,10 +597,9 @@
         rows = pl.ds(128 * q, 128)
         written.append(load(total_g.at[rows], parts.at[rows]))
 
-    waited = [w_up, w_dn, w_up2, w_dn2, *w_sib, t_up, t_dn, t_up1, t_dn1, t_up2, t_dn2, *rs_t]
-    for copy in sends:
-        if not any(copy is w for w in waited):
-            copy.wait_send()
+    for group in groups:
+        if group not in ("t", "w", "r"):
+            sent(group)
     for copy in written:
         copy.wait()
 
@@ -560,13 +640,12 @@
 ):
     tokens_all = teacher_in.shape[0] * lax.axis_size("context")
     smem = pl.BlockSpec(memory_space=pltpu.SMEM)
-    vmem = pl.BlockSpec(memory_space=pltpu.VMEM)
     hbm = pl.BlockSpec(memory_space=pl.ANY)
     parts = pl.pallas_call(
         functools.partial(kernel, tokens_all),
         name="distill",
         out_shape=jax.ShapeDtypeStruct((264, 1024), F32),
-        in_specs=[smem, smem, vmem, vmem, hbm, hbm, hbm, hbm, hbm],
+        in_specs=[smem, smem] + [hbm] * 7,
         out_specs=hbm,
         scratch_shapes=[
             pltpu.VMEM((1024, 2048), BF16),
@@ -580,9 +659,9 @@
             pltpu.VMEM((1024, 1024), BF16),
             pltpu.VMEM((1024, 1024), BF16),
             pltpu.VMEM((128, 4096), BF16),
-            pltpu.VMEM((64, 8192), BF16),
+            pltpu.VMEM((32, 8192), BF16),
             pltpu.VMEM((1024, 128), F32),
-            pltpu.VMEM((8, 8, 1024), F32),
+            pltpu.VMEM((8, 8, 128), F32),
             pltpu.VMEM((19, 8, 128), F32),
             pltpu.VMEM((8, 256, 1024), BF16),
             pltpu.VMEM((4, 256, ACOLS), BF16),
@@ -592,9 +671,11 @@
             pltpu.VMEM((2, 128, ACOLS), BF16),
             pltpu.VMEM((4, 128, 1024 - ACOLS), BF16),
             pltpu.VMEM((256, 1024), F32),
-            pltpu.SemaphoreType.DMA((COPIES,)),
-            pltpu.SemaphoreType.DMA((COPIES,)),
-            pltpu.SemaphoreType.DMA((10,)),
+            pltpu.VMEM((1, 4096), F32),
+            pltpu.VMEM((1, 1024), F32),
+            pltpu.SemaphoreType.DMA((SEND_SEMS,)),
+            pltpu.SemaphoreType.DMA((RECV_SEMS,)),
+            pltpu.SemaphoreType.DMA((11,)),
         ],
         compiler_params=pltpu.CompilerParams(
             collective_id=0, has_side_effects=True, vmem_limit_bytes=62 << 20

time: 161 us -> 156 us (0.969)
  Pallas kernels: 160 us -> 155 us
    pallas_call x1, Pallas kernels: 157 us -> 152 us  [local(): pl.pallas_call(functools.partial(kernel, tokens_all), name='distill', out...]
where the time goes in v4:
time: 156 us
  Pallas kernels  155 us (99%)
    pallas_call x1, Pallas kernels, local(): pl.pallas_call(functools.partial(kernel, tokens_all), name='distill', out...  152 us
    pallas_call x1, Pallas kernels, local(): pl.pallas_call(functools.partial(results, tokens_all), name='results', ou...  3.2 us

profile of v4, /device:TPU:0, one launch (start us, length us, event | category | flops | bytes accessed | tf_op | source)
XLA Modules:
  0.0 155.5 jit_solution(10139166257226282784)
XLA Ops:
  0.6 151.7 %distill.1.parts = f32[264,1024]{1,0:T(8,128)} custom-call(f32[16]{0:T(128)} %hist_in.3, f32[16]{0:T(128)} %hist_w.3, f32[1,4096]{1,0:T(1,128)} %bitcast.4, f32[1,8192]{1,0:T(1,128)} %bitcast.3, bf16[1024,512]{1,0:T(8,128)(2,1)} %tin.1, bf16[1024,1024]{1,0:T(8,128)(2,1)} %resid.1, bf16[512,8192]{1,0:T(8,128)(2,1)} %wo.1, bf16[128,4096]{1,0:T(8,128)(2,1)} %stu.1, ...), custom_call_target="tpu_custom_call" | custom-call | flops 25769803776 | bytes 16777216 | tf_op jit(solution)/shard_map/distill/pallas_call | solution.py:644
  152.3 3.2 %results.1 = (f32[256,1024]{1,0:T(8,128)}, f32[1]{0:T(128)}, f32[16]{0:T(128)}, f32[16]{0:T(128)}) custom-call(f32[264,1024]{1,0:T(8,128)} %distill.1.parts, f32[16]{0:T(128)} %hist_in.3, f32[16]{0:T(128)} %hist_w.3), custom_call_target="tpu_custom_call" | custom-call | tf_op jit(solution)/shard_map/results/pallas_call | solution.py:697

commit v5 on v4

--- a/solution.py
+++ b/solution.py
@@ -14,7 +14,8 @@
 SEND_SEMS, RECV_SEMS = 7, 84
 GROUP = 8 << 20
 XROWS = 112
-ACOLS = 384
+FIRST = 80
+AROWS = 112
 
 
 def lanes(tile):
@@ -37,9 +38,9 @@
 
 def kernel(
     tokens_all,
-    hist_in, hist_w, stu_gain, tea_gain, tin, resid, wo, stu, proj,
+    hist_in_all, hist_w_all, stu_gain, tea_gain, tin, resid, wo, stu, proj,
     parts,
-    T, W, S, PR, R, H, M, E, psend, precv, sraw, wraw, col, sq, scal, sib, ra1, ra2, rb1, rb2, am, bm, total_g, sgain, tgain,
+    T, W, S, PR, R, H, M, E, psend, precv, sraw, wraw, col, sq, scal, sib, ra1, ra2, rb1, rb2, am, bm, total_g, sgain, tgain, hist_in, hist_w,
     ssem, rsem, lsem,
 ):
     t, c = lax.axis_index("tensor"), lax.axis_index("context")
@@ -118,6 +119,7 @@
 
     slab = pl.multiple_of(64 * (2 * z + k) + 32 * xh, 32)
     l_wraw = load(wo.at[pl.ds(slab, 32)], wraw)
+    l_hist = load(hist_in_all, hist_in), load(hist_w_all, hist_w)
     l_sgain = load(stu_gain, sgain)
     l_tgain = load(tea_gain.at[:, pl.ds(pl.multiple_of(1024 * t, 1024), 1024)], tgain)
     l_proj = load(proj, PR.at[pl.ds(pl.multiple_of(256 * c, 256), 256)])
@@ -133,6 +135,8 @@
         pl.semaphore_signal(barrier, 1, device_id=dev(dxh=dx, dz=dz), device_id_type=MESH)
     pl.semaphore_signal(barrier, 1, device_id=dev(dk=1), device_id_type=MESH)
 
+    for copy in l_hist:
+        copy.wait()
     lim_in, lim_w = hist_in[0], hist_w[0]
     for i in range(1, 16):
         lim_in = jnp.maximum(lim_in, hist_in[i])
@@ -165,6 +169,7 @@
         at = ((xh + dxh) % 2) * 8 + ((z + dz) % 4) * 2 + k
         return PR.at[pl.ds(pl.multiple_of(256 * at, 256), 256)]
 
+    p_x = send(pblock(), pblock(), dxh=1)
     p_up = send(pblock(), pblock(), dz=UP)
     p_dn = send(pblock(), pblock(), dz=DOWN)
     p_sib = [send(pblock(), pblock(), dk=1)]
@@ -217,7 +222,6 @@
     w_up = send(wslab(0, 0), wslab(0, 0), "w", dz=UP)
     w_dn = send(wslab(0, 0), wslab(0, 0), "w", dz=DOWN)
     sx = send(S.at[0, own_x], S.at[0, far_x], dxl=1)
-    p_x = send(pblock(), pblock(), dxh=1)
 
     l_wown.wait()
 
@@ -262,6 +266,10 @@
     w_up2.wait_recv()
     v_dn2.wait_recv()
     w_sib.append(send(wslab(2), wslab(2), "w", dk=1))
+    p_x.wait_recv()
+    p_sib.append(send(pblock(1), pblock(1), dk=1))
+    q_dn = send(pblock(1), pblock(1), dz=DOWN)
+    q_up = send(pblock(1), pblock(1), dz=UP)
     p_up.wait_recv()
     p_up2 = send(pblock(0, DOWN), pblock(0, DOWN), dz=UP)
     p_sib.append(send(pblock(0, DOWN), pblock(0, DOWN), dk=1))
@@ -287,11 +295,6 @@
 
         for rows in (rows,) if q < 3 else (pl.ds(768, 128), pl.ds(896, 128)):
             rs_t.append(send(psend.at[rows], precv.at[rows], "r", dxl=1))
-        if q == 0:
-            p_x.wait_recv()
-            p_sib.append(send(pblock(1), pblock(1), dk=1))
-            q_dn = send(pblock(1), pblock(1), dz=DOWN)
-            q_up = send(pblock(1), pblock(1), dz=UP)
 
 
     sy_up2.wait_recv()
@@ -313,11 +316,12 @@
     p_sib.append(send(pblock(1, DOWN), pblock(1, DOWN), dk=1))
     p_up2.wait_recv()
     p_sib.append(send(pblock(0, 2), pblock(0, 2), dk=1))
-    parts_x = [(pl.ds(0, 64), pl.ds(64, nx - 64)), (pl.ds(128, 64), pl.ds(192, nx - 64))]
+    first_x = pl.ds(0, FIRST), pl.ds(128, FIRST)
+    last_x = pl.ds(FIRST, nx - FIRST), pl.ds(128 + FIRST, nx - FIRST)
     a_up.wait_recv()
-    a_up2, a_up3 = [send(S.at[3, rows], S.at[2, rows], dy=UP) for rows in parts_x[0]]
+    a_up2 = send(S.at[3, first_x[0]], S.at[2, first_x[0]], dy=UP)
     b_dn.wait_recv()
-    b_dn2, b_dn3 = [send(S.at[1, rows], S.at[2, rows], dy=DOWN) for rows in parts_x[1]]
+    b_dn2 = send(S.at[1, first_x[1]], S.at[2, first_x[1]], dy=DOWN)
     q_dn2.wait_recv()
     p_sib.append(send(pblock(1, 2), pblock(1, 2), dk=1))
 
@@ -329,14 +333,15 @@
                 S[r], PR[:, cols], preferred_element_type=F32
             )
 
-    def mapped_part(first):
+    def mapped_part(first, count):
         @pl.loop(0, 2)
         def _(n):
             cols = pl.ds(pl.multiple_of(512 * n, 512), 512)
-            rows = jnp.concatenate([S[2, pl.ds(first, 64)], S[2, pl.ds(128 + first, 64)]], axis=0)
+            own, far = pl.ds(first, count), pl.ds(128 + first, count)
+            rows = jnp.concatenate([S[2, own], S[2, far]], axis=0)
             out = jnp.dot(rows, PR[:, cols], preferred_element_type=F32)
-            M[pl.ds(512 + first, 64), cols] = out[:64]
-            M[pl.ds(640 + first, 64), cols] = out[64:]
+            M[pl.ds(512 + first, count), cols] = out[:count]
+            M[pl.ds(640 + first, count), cols] = out[count:]
 
     ORDER = [(1, 2), (0, 2), (1, 1), (1, 3), (1, 0), (0, 1), (0, 3), (0, 0)]
 
@@ -397,6 +402,8 @@
     sq_c = send_all(
         [(sq.at[0], sq.at[dy * 2 + dx], {"dy": dy, "dxl": dx}) for dy, dx in TENSOR], "s"
     )
+    a_up3 = send(S.at[3, last_x[0]], S.at[2, last_x[0]], dy=UP)
+    b_dn3 = send(S.at[1, last_x[1]], S.at[2, last_x[1]], dy=DOWN)
     turn_first(1)
 
     def errors(r, acc):
@@ -411,16 +418,12 @@
                 E[here, :] = e.astype(BF16)
                 return acc + fold(jnp.add, e * e)
 
-            acc = lax.fori_loop(0, 8, step, acc)
+            acc = lax.fori_loop(0, 8, step, acc, unroll=2)
         return acc
 
     a_up2.wait_recv()
     b_dn2.wait_recv()
-    mapped_part(0)
-    sxy[3].wait_recv()
-    a_up3.wait_recv()
-    b_dn3.wait_recv()
-    mapped_part(64)
+    mapped_part(0, FIRST)
     await_group(sq_c)
     total = sq[0]
     for i in range(1, 8):
@@ -429,8 +432,13 @@
     for i in range(8):
         col[pl.ds(128 * i, 128), :] = jnp.broadcast_to(inv[i : i + 1, :], (128, 128)).T
     acc = jnp.zeros((8, 128), F32)
-    for r in range(4):
+    for r in (0, 3, 1):
         acc = errors(r, acc)
+    sxy[3].wait_recv()
+    a_up3.wait_recv()
+    b_dn3.wait_recv()
+    mapped_part(FIRST, 128 - FIRST)
+    acc = errors(2, acc)
 
     tile = jnp.where(row == 0, jnp.max(amax_in), jnp.where(row == 1, jnp.max(amax_w), jnp.sum(acc)))
 
@@ -447,35 +455,37 @@
     sent("w")
     sent("r")
 
-    a_cols, b_cols = pl.ds(0, ACOLS), pl.ds(ACOLS, 1024 - ACOLS)
-
-    def gslot(dxh, dz, cols, first=0, count=256):
+    a_rows, b_rows = (0, AROWS), (AROWS, 256 - AROWS)
+    a_up_rows, a_dn_rows = (0, 48), (48, AROWS - 48)
+    b_up_rows, b_dn_rows = (AROWS, 80), (AROWS + 80, 176 - AROWS)
+
+    def gslot(dxh, dz, rows=(0, 256), other=0):
         g = ORDER.index((dxh, dz))
-        return W.at[g // 2, pl.ds(256 * (g % 2) + first, count), cols]
+        return W.at[g // 2, pl.ds(256 * (g % 2) + rows[0], rows[1]), pl.ds(1024 * other, 1024)]
 
     to_sib, a_1, b_1, a_2, a_m, b_m = [], {}, {}, {}, {}, {}
+
+    def half_term(g, own):
+        dxh, dz = ORDER[g]
+        ref, row0, col0 = turned(g)
+
+        @pl.loop(0, 2)
+        def _(n):
+            at = pl.multiple_of(512 * n, 512)
+            one = jnp.dot(
+                ref[pl.ds(row0 + 256 * own, 256), pl.ds(col0, 1024)],
+                E[:, pl.ds(at, 512)],
+                preferred_element_type=F32,
+            )
+            start = pl.multiple_of(1024 * (1 - own) + at, 512)
+            W[g // 2, pl.ds(256 * (g % 2), 256), pl.ds(start, 512)] = one.astype(BF16)
+
+        if own == 0:
+            to_sib.append(send(gslot(dxh, dz, other=1), sib.at[g], dk=1))
 
     def term(g):
         dxh, dz = ORDER[g]
         ref, row0, col0 = turned(g)
-
-        if g == 0:
-            for own in (0, 1):
-
-                @pl.loop(0, 2)
-                def _(n):
-                    at = pl.multiple_of(512 * n, 512)
-                    one = jnp.dot(
-                        ref[pl.ds(row0 + 256 * own, 256), pl.ds(col0, 1024)],
-                        E[:, pl.ds(at, 512)],
-                        preferred_element_type=F32,
-                    )
-                    start = pl.multiple_of(1024 * (1 - own) + at, 512)
-                    W[0, pl.ds(0, 256), pl.ds(start, 512)] = one.astype(BF16)
-
-                if own == 0:
-                    to_sib.append(send(gslot(dxh, dz, pl.ds(1024, 1024)), sib.at[g], dk=1))
-            return
 
         @pl.loop(0, 2)
         def _(n):
@@ -489,54 +499,57 @@
             W[g // 2, rows, pl.ds(pl.multiple_of(1024 + at, 512), 512)] = both[:256]
             W[g // 2, rows, pl.ds(at, 512)] = both[256:]
 
-        to_sib.append(send(gslot(dxh, dz, pl.ds(1024, 1024)), sib.at[g], dk=1))
-
-    def add(dxh, dz, cols, others, first=0, count=256):
+        to_sib.append(send(gslot(dxh, dz, other=1), sib.at[g], dk=1))
+
+    def add(dxh, dz, rows, others):
         g = ORDER.index((dxh, dz))
 
-        @pl.loop(0, count // 16)
+        @pl.loop(0, rows[1] // 16)
         def _(i):
             here = pl.ds(pl.multiple_of(16 * i, 16), 16)
-            there = pl.ds(pl.multiple_of(first + 16 * i, 16), 16)
-            rows = pl.ds(pl.multiple_of(256 * (g % 2) + first + 16 * i, 16), 16)
-            total = W[g // 2, rows, cols].astype(F32)
-            for ref, index, whole in others:
-                total = total + ref[index, there if whole else here, :].astype(F32)
-            W[g // 2, rows, cols] = total.astype(BF16)
-
-    def along_z(dxh, dz, cols, mid, at, far, sent, passed):
+            there = pl.ds(pl.multiple_of(256 * (g % 2) + rows[0] + 16 * i, 16), 16)
+            total = W[g // 2, there, pl.ds(0, 1024)].astype(F32)
+            for ref, index in others:
+                total = total + ref[index, here, :].astype(F32)
+            W[g // 2, there, pl.ds(0, 1024)] = total.astype(BF16)
+
+    def along_z(dxh, dz, rows, up, dn, mid, at, far, gone, passed):
         if dz == 2:
-            passed[dxh, UP] = send(gslot(dxh, 2, cols, 0, 128), mid.at[at], dz=UP)
-            passed[dxh, DOWN] = send(gslot(dxh, 2, cols, 128, 128), mid.at[at + 1], dz=DOWN)
+            passed[dxh, UP] = send(gslot(dxh, 2, up), mid.at[at, pl.ds(0, up[1])], dz=UP)
+            passed[dxh, DOWN] = send(gslot(dxh, 2, dn), mid.at[at + 1, pl.ds(0, dn[1])], dz=DOWN)
         elif dz:
             passed[dxh, dz].wait_recv()
-            add(dxh, dz, cols, [(mid, at + dz // 2, False)], 64 * (dz - 1), 128)
-            sent[dxh, dz] = send(gslot(dxh, dz, cols), far.at[at + dz // 2], dz=dz)
+            add(dxh, dz, up if dz == UP else dn, [(mid, at + dz // 2)])
+            gone[dxh, dz] = send(gslot(dxh, dz, rows), far.at[at + dz // 2], dz=dz)
 
     def finish(g):
         dxh, dz = ORDER[g]
         to_sib[g].wait_recv()
-        add(dxh, dz, pl.ds(0, 1024), [(sib, g, True)])
+        add(dxh, dz, (0, 256), [(sib, g)])
         if dxh:
-            a_1[dz] = send(gslot(dxh, dz, a_cols), ra1.at[dz], dxh=1)
+            a_1[dz] = send(gslot(dxh, dz, a_rows), ra1.at[dz], dxh=1)
 
     def second_b(dxh, dz):
-        along_z(dxh, dz, b_cols, bm, 2 * dxh, rb1, b_1, b_m)
+        along_z(dxh, dz, b_rows, b_up_rows, b_dn_rows, bm, 2 * dxh, rb1, b_1, b_m)
 
     def second_a(dz):
         a_1[dz].wait_recv()
-        add(0, dz, a_cols, [(ra1, dz, True)])
-        along_z(0, dz, a_cols, am, 0, ra2, a_2, a_m)
+        add(0, dz, a_rows, [(ra1, dz)])
+        along_z(0, dz, a_rows, a_up_rows, a_dn_rows, am, 0, ra2, a_2, a_m)
 
     def term_of(g):
         for r in range(4) if g >= 4 else (2,):
             turn(g, r)
         term(g)
 
-    term_of(0)
-    term_of(1)
+    turn(0, 2)
+    half_term(0, 0)
+    half_term(0, 1)
+    turn(1, 2)
+    half_term(1, 0)
     finish(0)
     second_b(1, 2)
+    half_term(1, 1)
     await_group(sc1)
     at = 8 + xh * 4 + z
     scal[at] = merge(0, 8)
@@ -561,8 +574,8 @@
     second_b(0, 3)
     for n in (UP, DOWN):
         b_1[1, n].wait_recv()
-    add(1, 0, b_cols, [(rb1, 2, True), (rb1, 3, True)])
-    b_2 = send(gslot(1, 0, b_cols), rb2.at[0], dxh=1)
+    add(1, 0, b_rows, [(rb1, 2), (rb1, 3)])
+    b_2 = send(gslot(1, 0, b_rows), rb2.at[0], dxh=1)
     second_a(1)
     second_a(3)
     await_group(sc2)
@@ -579,24 +592,24 @@
         a_2[0, n].wait_recv()
     b_2.wait_recv()
     scale = 1.0 / math.sqrt(tokens_all)
-    for q in range(2):
-
-        @pl.loop(0, 8)
+    for (first, count), landed in (
+        (b_rows, [(rb1, 0), (rb1, 1), (rb2, 0)]),
+        (a_rows, [(ra2, 0), (ra2, 1)]),
+    ):
+
+        @pl.loop(0, count // 16)
         def _(i):
-            rows = pl.ds(pl.multiple_of(128 * q + 16 * i, 16), 16)
-            mine = pl.ds(pl.multiple_of(256 + 128 * q + 16 * i, 16), 16)
-            total = W[3, mine, a_cols].astype(F32)
-            for n in range(2):
-                total = total + ra2[n, rows, :].astype(F32)
-            total_g[rows, a_cols] = total * scale
-            total = W[3, mine, b_cols].astype(F32) + rb2[0, rows, :].astype(F32)
-            for n in range(2):
-                total = total + rb1[n, rows, :].astype(F32)
-            total_g[rows, b_cols] = total * scale
-
-        rows = pl.ds(128 * q, 128)
+            here = pl.ds(pl.multiple_of(16 * i, 16), 16)
+            mine = pl.ds(pl.multiple_of(256 + first + 16 * i, 16), 16)
+            total = W[3, mine, pl.ds(0, 1024)].astype(F32)
+            for ref, index in landed:
+                total = total + ref[index, here, :].astype(F32)
+            total_g[pl.ds(pl.multiple_of(first + 16 * i, 16), 16), :] = total * scale
+
+        rows = pl.ds(first, count)
         written.append(load(total_g.at[rows], parts.at[rows]))
 
+    assert len(groups) <= SEND_SEMS and len(received) <= RECV_SEMS
     for group in groups:
         if group not in ("t", "w", "r"):
             sent(group)
@@ -605,32 +618,40 @@
 
 
 def results(
-    tokens_all, parts, hist_in, hist_w, grad, loss, hist_in_new, hist_w_new, held, tile, sem_in, sem_out
+    tokens_all, parts, hist_in, hist_w, grad, loss, hist_in_new, hist_w_new,
+    held, tile, s_in, s_w, s_in_new, s_w_new, s_loss, sem_in, sem_out,
 ):
-    scalars = pltpu.make_async_copy(parts.at[pl.ds(256, 8), pl.ds(0, 128)], tile, sem_in.at[4])
-    scalars.start()
     pieces = [pl.ds(64 * i, 64) for i in range(4)]
-    ins = [
-        pltpu.make_async_copy(parts.at[rows], held.at[rows], sem_in.at[i])
-        for i, rows in enumerate(pieces)
+    copies = [
+        (parts.at[pl.ds(256, 8), pl.ds(0, 128)], tile),
+        (hist_in, s_in),
+        (hist_w, s_w),
+        *((parts.at[rows], held.at[rows]) for rows in pieces),
     ]
-    outs = [
-        pltpu.make_async_copy(held.at[rows], grad.at[rows], sem_out.at[i])
-        for i, rows in enumerate(pieces)
+    copies = [pltpu.make_async_copy(a, b, sem_in.at[i]) for i, (a, b) in enumerate(copies)]
+    for copy in copies:
+        copy.start()
+    backs = [
+        *((held.at[rows], grad.at[rows]) for rows in pieces),
+        (s_in_new, hist_in_new),
+        (s_w_new, hist_w_new),
+        (s_loss, loss),
     ]
-    for copy in ins:
-        copy.start()
+    backs = [pltpu.make_async_copy(a, b, sem_out.at[i]) for i, (a, b) in enumerate(backs)]
+    for copy in copies[:3]:
+        copy.wait()
+    s_in_new[0] = jnp.max(tile[0:1, :])
+    s_w_new[0] = jnp.max(tile[1:2, :])
+    s_loss[0] = jnp.max(tile[2:3, :]) * (0.5 / (tokens_all * 8192))
     for i in range(15):
-        hist_in_new[i + 1] = hist_in[i]
-        hist_w_new[i + 1] = hist_w[i]
-    for copy, back in zip(ins, outs):
+        s_in_new[i + 1] = s_in[i]
+        s_w_new[i + 1] = s_w[i]
+    for back in backs[4:]:
+        back.start()
+    for copy, back in zip(copies[3:], backs):
         copy.wait()
         back.start()
-    scalars.wait()
-    hist_in_new[0] = jnp.max(tile[0:1, :])
-    hist_w_new[0] = jnp.max(tile[1:2, :])
-    loss[0] = jnp.max(tile[2:3, :]) * (0.5 / (tokens_all * 8192))
-    for back in outs:
+    for back in backs:
         back.wait()
 
 
@@ -639,13 +660,12 @@
     student_hidden, student_gain, projection,
 ):
     tokens_all = teacher_in.shape[0] * lax.axis_size("context")
-    smem = pl.BlockSpec(memory_space=pltpu.SMEM)
     hbm = pl.BlockSpec(memory_space=pl.ANY)
     parts = pl.pallas_call(
         functools.partial(kernel, tokens_all),
         name="distill",
         out_shape=jax.ShapeDtypeStruct((264, 1024), F32),
-        in_specs=[smem, smem] + [hbm] * 7,
+        in_specs=[hbm] * 9,
         out_specs=hbm,
         scratch_shapes=[
             pltpu.VMEM((1024, 2048), BF16),
@@ -664,18 +684,20 @@
             pltpu.VMEM((8, 8, 128), F32),
             pltpu.VMEM((19, 8, 128), F32),
             pltpu.VMEM((8, 256, 1024), BF16),
-            pltpu.VMEM((4, 256, ACOLS), BF16),
-            pltpu.VMEM((2, 256, ACOLS), BF16),
-            pltpu.VMEM((4, 256, 1024 - ACOLS), BF16),
-            pltpu.VMEM((1, 256, 1024 - ACOLS), BF16),
-            pltpu.VMEM((2, 128, ACOLS), BF16),
-            pltpu.VMEM((4, 128, 1024 - ACOLS), BF16),
+            pltpu.VMEM((4, AROWS, 1024), BF16),
+            pltpu.VMEM((2, AROWS, 1024), BF16),
+            pltpu.VMEM((4, 256 - AROWS, 1024), BF16),
+            pltpu.VMEM((1, 256 - AROWS, 1024), BF16),
+            pltpu.VMEM((2, 64, 1024), BF16),
+            pltpu.VMEM((4, 80, 1024), BF16),
             pltpu.VMEM((256, 1024), F32),
             pltpu.VMEM((1, 4096), F32),
             pltpu.VMEM((1, 1024), F32),
+            pltpu.SMEM((16,), F32),
+            pltpu.SMEM((16,), F32),
             pltpu.SemaphoreType.DMA((SEND_SEMS,)),
             pltpu.SemaphoreType.DMA((RECV_SEMS,)),
-            pltpu.SemaphoreType.DMA((11,)),
+            pltpu.SemaphoreType.DMA((13,)),
         ],
         compiler_params=pltpu.CompilerParams(
             collective_id=0, has_side_effects=True, vmem_limit_bytes=62 << 20
@@ -703,13 +725,14 @@
             jax.ShapeDtypeStruct((16,), F32),
             jax.ShapeDtypeStruct((16,), F32),
         ),
-        in_specs=[hbm, smem, smem],
-        out_specs=(hbm, smem, smem, smem),
+        in_specs=[hbm] * 3,
+        out_specs=(hbm,) * 4,
         scratch_shapes=[
             pltpu.VMEM((256, 1024), F32),
             pltpu.VMEM((8, 128), F32),
-            pltpu.SemaphoreType.DMA((5,)),
-            pltpu.SemaphoreType.DMA((4,)),
+            *(pltpu.SMEM((n,), F32) for n in (16, 16, 16, 16, 1)),
+            pltpu.SemaphoreType.DMA((7,)),
+            pltpu.SemaphoreType.DMA((7,)),
         ],
     )(parts, input_history, weight_history)
     return grad, loss.reshape(()), hist_in, hist_w

time: 156 us -> 153 us (0.981)
  Pallas kernels: 155 us -> 152 us
    pallas_call x1, Pallas kernels: 152 us -> 150 us  [local(): pl.pallas_call(functools.partial(kernel, tokens_all), name='distill', out...]
where the time goes in v5:
time: 153 us; the launch traced here: 152 us
  Pallas kernels  152 us (99%)
    pallas_call x1, Pallas kernels, local(): pl.pallas_call(functools.partial(kernel, tokens_all), name='distill', out...  150 us

profile of v5, /device:TPU:0, one launch (start us, length us, event | category | flops | bytes accessed | tf_op | source)
XLA Modules:
  0.0 152.4 jit_solution(5261530587810287459)
XLA Ops:
  0.6 149.7 %distill.1.parts = f32[264,1024]{1,0:T(8,128)} custom-call(f32[16]{0:T(128)} %hist_in.1, f32[16]{0:T(128)} %hist_w.1, f32[1,4096]{1,0:T(1,128)} %bitcast.4, f32[1,8192]{1,0:T(1,128)} %bitcast.3, bf16[1024,512]{1,0:T(8,128)(2,1)} %tin.1, bf16[1024,1024]{1,0:T(8,128)(2,1)} %resid.1, bf16[512,8192]{1,0:T(8,128)(2,1)} %wo.1, bf16[128,4096]{1,0:T(8,128)(2,1)} %stu.1, ...), custom_call_target="tpu_custom_call" | custom-call | flops 25769803776 | bytes 16777216 | tf_op jit(solution)/shard_map/distill/pallas_call | solution.py:664
  150.4 2.1 %results.1 = (f32[256,1024]{1,0:T(8,128)}, f32[1]{0:T(128)}, f32[16]{0:T(128)}, f32[16]{0:T(128)}) custom-call(f32[264,1024]{1,0:T(8,128)} %distill.1.parts, f32[16]{0:T(128)} %hist_in.1, f32[16]{0:T(128)} %hist_w.1), custom_call_target="tpu_custom_call" | custom-call | tf_op jit(solution)/shard_map/results/pallas_call | solution.py:719

commit v6 on v5

--- a/solution.py
+++ b/solution.py
@@ -11,10 +11,10 @@
 MESH = pl.DeviceIdType.MESH
 F32, BF16 = jnp.float32, jnp.bfloat16
 EPS = 1e-05
-SEND_SEMS, RECV_SEMS = 7, 84
+SEND_SEMS, RECV_SEMS = 7, 88
 GROUP = 8 << 20
-XROWS = 112
-FIRST = 80
+XCOLS = 3456
+PIECES = (0, 1408), (1408, 1408), (2816, 640)
 AROWS = 112
 
 
@@ -184,13 +184,12 @@
         mean = jnp.mean(v * v, axis=1, keepdims=True)
         S[0, rows, :] = (v * lax.rsqrt(mean + EPS) * sgain[...]).astype(BF16)
 
-    nx = XROWS
-    ny = 128 - nx
-    own_x, own_y = pl.ds(0, nx), pl.ds(nx, ny)
-    far_x, far_y = pl.ds(128, nx), pl.ds(128 + nx, ny)
-    sy_up = send(S.at[0, own_y], S.at[3, own_y], dy=UP)
-    sy_dn = send(S.at[0, own_y], S.at[1, own_y], dy=DOWN)
-    sxy = [send(S.at[0, own_y], S.at[0, far_y], dxl=1)]
+    own, far = pl.ds(0, 128), pl.ds(128, 128)
+    x_cols, y_cols = pl.ds(0, XCOLS), pl.ds(XCOLS, 4096 - XCOLS)
+    own_x, own_y, far_x, far_y = (own, x_cols), (own, y_cols), (far, x_cols), (far, y_cols)
+    sy_up = send(S.at[0, *own_y], S.at[3, *own_y], dy=UP)
+    sy_dn = send(S.at[0, *own_y], S.at[1, *own_y], dy=DOWN)
+    sxy = [send(S.at[0, *own_y], S.at[0, *far_y], dxl=1)]
 
     l_tin.wait()
 
@@ -221,7 +220,7 @@
     w_x = send(wslab(0, 0), wslab(0, 0), "w", dxh=1)
     w_up = send(wslab(0, 0), wslab(0, 0), "w", dz=UP)
     w_dn = send(wslab(0, 0), wslab(0, 0), "w", dz=DOWN)
-    sx = send(S.at[0, own_x], S.at[0, far_x], dxl=1)
+    sx = send(S.at[0, *own_x], S.at[0, *far_x], dxl=1)
 
     l_wown.wait()
 
@@ -232,22 +231,22 @@
         W[0, rows, :] = jnp.clip(v, -lim_w, lim_w).astype(BF16)
 
     sy_up.wait_recv()
-    sxy.append(send(S.at[3, own_y], S.at[3, far_y], dxl=1))
+    sxy.append(send(S.at[3, *own_y], S.at[3, *far_y], dxl=1))
     sy_dn.wait_recv()
-    sxy.append(send(S.at[1, own_y], S.at[1, far_y], dxl=1))
+    sxy.append(send(S.at[1, *own_y], S.at[1, *far_y], dxl=1))
     w_x.wait_recv()
     v_dn = send(wslab(0, 1), wslab(0, 1), "w", dz=DOWN)
     v_up = send(wslab(0, 1), wslab(0, 1), "w", dz=UP)
     w_sib = [send(wslab(), wslab(), "w", dk=1)]
 
-    left, right = pl.ds(0, 2048), pl.ds(2048, 2048)
+    upper, lower = (pl.ds(0, 64), y_cols), (pl.ds(64, 64), y_cols)
     t_up.wait_recv()
     t_up2 = send(tblock(3, low), tblock(2, low), "t", dy=UP)
     t_dn.wait_recv()
     t_dn2 = send(tblock(1, high), tblock(2, high), "t", dy=DOWN)
-    sy_up2 = send(S.at[3, own_y, left], S.at[2, own_y, left], dy=UP)
-    sy_dn2 = send(S.at[1, own_y, right], S.at[2, own_y, right], dy=DOWN)
-    a_up = send(S.at[0, own_x], S.at[3, own_x], dy=UP)
+    sy_up2 = send(S.at[3, *upper], S.at[2, *upper], dy=UP)
+    sy_dn2 = send(S.at[1, *lower], S.at[2, *lower], dy=DOWN)
+    a_up = send(S.at[0, *own_x], S.at[3, *own_x], dy=UP)
 
     w_up.wait_recv()
     w_up2 = send(wslab(DOWN, 0), wslab(DOWN, 0), "w", dz=UP)
@@ -259,9 +258,9 @@
     w_sib.append(send(wslab(UP), wslab(UP), "w", dk=1))
 
     sx.wait_recv()
-    b_dn = send(S.at[0, far_x], S.at[1, far_x], dy=DOWN)
-    b_up = send(S.at[0, far_x], S.at[3, far_x], dy=UP)
-    a_dn = send(S.at[0, own_x], S.at[1, own_x], dy=DOWN)
+    b_dn = send(S.at[0, *far_x], S.at[1, *far_x], dy=DOWN)
+    b_up = send(S.at[0, *far_x], S.at[3, *far_x], dy=UP)
+    a_dn = send(S.at[0, *own_x], S.at[1, *own_x], dy=DOWN)
 
     w_up2.wait_recv()
     v_dn2.wait_recv()
@@ -299,7 +298,7 @@
 
     sy_up2.wait_recv()
     sy_dn2.wait_recv()
-    sxy.append(send(S.at[2, own_y], S.at[2, far_y], dxl=1))
+    sxy.append(send(S.at[2, *own_y], S.at[2, *far_y], dxl=1))
     l_res.wait()
     for q in range(4):
         rows = pl.ds(256 * q, 256)
@@ -316,12 +315,11 @@
     p_sib.append(send(pblock(1, DOWN), pblock(1, DOWN), dk=1))
     p_up2.wait_recv()
     p_sib.append(send(pblock(0, 2), pblock(0, 2), dk=1))
-    first_x = pl.ds(0, FIRST), pl.ds(128, FIRST)
-    last_x = pl.ds(FIRST, nx - FIRST), pl.ds(128 + FIRST, nx - FIRST)
+    first, second, last = [pl.ds(*piece) for piece in PIECES]
     a_up.wait_recv()
-    a_up2 = send(S.at[3, first_x[0]], S.at[2, first_x[0]], dy=UP)
+    a_up2, a_up3 = [send(S.at[3, own, n], S.at[2, own, n], dy=UP) for n in (first, second)]
     b_dn.wait_recv()
-    b_dn2 = send(S.at[1, first_x[1]], S.at[2, first_x[1]], dy=DOWN)
+    b_dn2, b_dn3 = [send(S.at[1, far, n], S.at[2, far, n], dy=DOWN) for n in (first, second)]
     q_dn2.wait_recv()
     p_sib.append(send(pblock(1, 2), pblock(1, 2), dk=1))
 
@@ -333,15 +331,12 @@
                 S[r], PR[:, cols], preferred_element_type=F32
             )
 
-    def mapped_part(first, count):
+    def mapped_part(inner, add_up):
         @pl.loop(0, 2)
         def _(n):
             cols = pl.ds(pl.multiple_of(512 * n, 512), 512)
-            own, far = pl.ds(first, count), pl.ds(128 + first, count)
-            rows = jnp.concatenate([S[2, own], S[2, far]], axis=0)
-            out = jnp.dot(rows, PR[:, cols], preferred_element_type=F32)
-            M[pl.ds(512 + first, count), cols] = out[:count]
-            M[pl.ds(640 + first, count), cols] = out[count:]
+            out = jnp.dot(S[2, :, inner], PR[inner, cols], preferred_element_type=F32)
+            M[pl.ds(512, 256), cols] = M[pl.ds(512, 256), cols] + out if add_up else out
 
     ORDER = [(1, 2), (0, 2), (1, 1), (1, 3), (1, 0), (0, 1), (0, 3), (0, 0)]
 
@@ -393,6 +388,9 @@
     sxy[2].wait_recv()
     mapped(1)
     squares(3)
+    a_up2.wait_recv()
+    b_dn2.wait_recv()
+    mapped_part(first, False)
     squares(4)
     row = lax.broadcasted_iota(jnp.int32, (8, 128), 0)
     packed = jnp.zeros((8, 128), F32)
@@ -402,8 +400,8 @@
     sq_c = send_all(
         [(sq.at[0], sq.at[dy * 2 + dx], {"dy": dy, "dxl": dx}) for dy, dx in TENSOR], "s"
     )
-    a_up3 = send(S.at[3, last_x[0]], S.at[2, last_x[0]], dy=UP)
-    b_dn3 = send(S.at[1, last_x[1]], S.at[2, last_x[1]], dy=DOWN)
+    a_up4 = send(S.at[3, own, last], S.at[2, own, last], dy=UP)
+    b_dn4 = send(S.at[1, far, last], S.at[2, far, last], dy=DOWN)
     turn_first(1)
 
     def errors(r, acc):
@@ -421,9 +419,9 @@
             acc = lax.fori_loop(0, 8, step, acc, unroll=2)
         return acc
 
-    a_up2.wait_recv()
-    b_dn2.wait_recv()
-    mapped_part(0, FIRST)
+    a_up3.wait_recv()
+    b_dn3.wait_recv()
+    mapped_part(second, True)
     await_group(sq_c)
     total = sq[0]
     for i in range(1, 8):
@@ -434,10 +432,20 @@
     acc = jnp.zeros((8, 128), F32)
     for r in (0, 3, 1):
         acc = errors(r, acc)
+
+    @pl.loop(0, 2)
+    def _(n):
+        cols = pl.ds(pl.multiple_of(512 * n, 512), 512)
+        M[pl.ds(0, 256), cols] = jnp.dot(
+            T[pl.ds(0, 256), pl.ds(0, 512)], E[pl.ds(0, 512), cols], preferred_element_type=F32
+        ) + jnp.dot(
+            T[pl.ds(0, 256), pl.ds(768, 256)], E[pl.ds(768, 256), cols], preferred_element_type=F32
+        )
+
     sxy[3].wait_recv()
-    a_up3.wait_recv()
-    b_dn3.wait_recv()
-    mapped_part(FIRST, 128 - FIRST)
+    a_up4.wait_recv()
+    b_dn4.wait_recv()
+    mapped_part(pl.ds(PIECES[2][0], 4096 - PIECES[2][0]), True)
     acc = errors(2, acc)
 
     tile = jnp.where(row == 0, jnp.max(amax_in), jnp.where(row == 1, jnp.max(amax_w), jnp.sum(acc)))
@@ -472,11 +480,13 @@
         @pl.loop(0, 2)
         def _(n):
             at = pl.multiple_of(512 * n, 512)
-            one = jnp.dot(
-                ref[pl.ds(row0 + 256 * own, 256), pl.ds(col0, 1024)],
-                E[:, pl.ds(at, 512)],
-                preferred_element_type=F32,
-            )
+            rows, cols = pl.ds(row0 + 256 * own, 256), pl.ds(at, 512)
+            if (g, own) == (0, 0):
+                one = M[rows, cols] + jnp.dot(
+                    ref[rows, pl.ds(512, 256)], E[pl.ds(512, 256), cols], preferred_element_type=F32
+                )
+            else:
+                one = jnp.dot(ref[rows, pl.ds(col0, 1024)], E[:, cols], preferred_element_type=F32)
             start = pl.multiple_of(1024 * (1 - own) + at, 512)
             W[g // 2, pl.ds(256 * (g % 2), 256), pl.ds(start, 512)] = one.astype(BF16)
 

time: 153 us -> 150 us (0.980)
  Pallas kernels: 152 us -> 150 us
    pallas_call x1, Pallas kernels: 150 us -> 148 us  [local(): pl.pallas_call(functools.partial(kernel, tokens_all), name='distill', out...]
where the time goes in v6:
time: 150 us
  Pallas kernels  150 us (100%)
    pallas_call x1, Pallas kernels, local(): pl.pallas_call(functools.partial(kernel, tokens_all), name='distill', out...  148 us

profile of v6, /device:TPU:0, one launch (start us, length us, event | category | flops | bytes accessed | tf_op | source)
XLA Modules:
  0.0 150.3 jit_solution(12497507501279103987)
XLA Ops:
  0.6 147.6 %distill.1.parts = f32[264,1024]{1,0:T(8,128)} custom-call(f32[16]{0:T(128)} %hist_in.1, f32[16]{0:T(128)} %hist_w.1, f32[1,4096]{1,0:T(1,128)} %bitcast.4, f32[1,8192]{1,0:T(1,128)} %bitcast.3, bf16[1024,512]{1,0:T(8,128)(2,1)} %tin.1, bf16[1024,1024]{1,0:T(8,128)(2,1)} %resid.1, bf16[512,8192]{1,0:T(8,128)(2,1)} %wo.1, bf16[128,4096]{1,0:T(8,128)(2,1)} %stu.1, ...), custom_call_target="tpu_custom_call" | custom-call | flops 25769803776 | bytes 16777216 | tf_op jit(solution)/shard_map/distill/pallas_call | solution.py:674
  148.2 2.1 %results.1 = (f32[256,1024]{1,0:T(8,128)}, f32[1]{0:T(128)}, f32[16]{0:T(128)}, f32[16]{0:T(128)}) custom-call(f32[264,1024]{1,0:T(8,128)} %distill.1.parts, f32[16]{0:T(128)} %hist_in.1, f32[16]{0:T(128)} %hist_w.1), custom_call_target="tpu_custom_call" | custom-call | tf_op jit(solution)/shard_map/results/pallas_call | solution.py:729

commit v7 on v6

--- a/solution.py
+++ b/solution.py
@@ -11,7 +11,7 @@
 MESH = pl.DeviceIdType.MESH
 F32, BF16 = jnp.float32, jnp.bfloat16
 EPS = 1e-05
-SEND_SEMS, RECV_SEMS = 7, 88
+SEND_SEMS, RECV_SEMS = 7, 73
 GROUP = 8 << 20
 XCOLS = 3456
 PIECES = (0, 1408), (1408, 1408), (2816, 640)
@@ -39,8 +39,8 @@
 def kernel(
     tokens_all,
     hist_in_all, hist_w_all, stu_gain, tea_gain, tin, resid, wo, stu, proj,
-    parts,
-    T, W, S, PR, R, H, M, E, psend, precv, sraw, wraw, col, sq, scal, sib, ra1, ra2, rb1, rb2, am, bm, total_g, sgain, tgain, hist_in, hist_w,
+    parts, ra2, rb2,
+    T, W, S, PR, R, H, M, E, psend, precv, sraw, wraw, col, sq, scal, sib, ra1, rb1, am, bm, total_g, sgain, tgain, hist_in, hist_w,
     ssem, rsem, lsem,
 ):
     t, c = lax.axis_index("tensor"), lax.axis_index("context")
@@ -67,13 +67,19 @@
     def size(ref):
         return math.prod(ref.shape) * jnp.dtype(ref.dtype).itemsize
 
-    def send(src, dst, group=None, **to):
+    landing = {}
+
+    def send(src, dst, group=None, land=None, **to):
         if group is None:
             group = next((n for n in range(50) if groups.get(n, (0, 0))[1] + size(src) <= GROUP), 0)
         index, held = groups.get(group, (len(groups), 0))
         groups[group] = index, held + size(src)
-        received.append(len(received))
-        copy = remote(src, dst, index, received[-1], dev(**to))
+        if land is None or land not in landing:
+            received.append(len(received))
+        at, total = landing.get(land, (received[-1], 0))
+        if land is not None:
+            landing[land] = at, total + size(src)
+        copy = remote(src, dst, index, at, dev(**to))
         copy.start()
         return copy
 
@@ -172,7 +178,7 @@
     p_x = send(pblock(), pblock(), dxh=1)
     p_up = send(pblock(), pblock(), dz=UP)
     p_dn = send(pblock(), pblock(), dz=DOWN)
-    p_sib = [send(pblock(), pblock(), dk=1)]
+    p_sib = [send(pblock(), pblock(), land="p", dk=1)]
 
     l_stu.wait()
     l_sgain.wait()
@@ -207,8 +213,8 @@
 
     t_up = send(tblock(0, low), tblock(3, low), "t", dy=UP)
     t_dn = send(tblock(0, high), tblock(1, high), "t", dy=DOWN)
-    t_up1 = send(tblock(0, high), tblock(3, high), "t", dy=UP)
-    t_dn1 = send(tblock(0, low), tblock(1, low), "t", dy=DOWN)
+    t_up1 = send(tblock(0, high), tblock(3, high), "t", "t", dy=UP)
+    t_dn1 = send(tblock(0, low), tblock(1, low), "t", "t", dy=DOWN)
 
     def wslab(dz=0, dxh=None):
         at = pl.multiple_of(64 * (2 * ((z + dz) % 4) + k), 64)
@@ -237,13 +243,13 @@
     w_x.wait_recv()
     v_dn = send(wslab(0, 1), wslab(0, 1), "w", dz=DOWN)
     v_up = send(wslab(0, 1), wslab(0, 1), "w", dz=UP)
-    w_sib = [send(wslab(), wslab(), "w", dk=1)]
+    w_sib = [send(wslab(), wslab(), "w", "w", dk=1)]
 
     upper, lower = (pl.ds(0, 64), y_cols), (pl.ds(64, 64), y_cols)
     t_up.wait_recv()
-    t_up2 = send(tblock(3, low), tblock(2, low), "t", dy=UP)
+    t_up2 = send(tblock(3, low), tblock(2, low), "t", "t", dy=UP)
     t_dn.wait_recv()
-    t_dn2 = send(tblock(1, high), tblock(2, high), "t", dy=DOWN)
+    t_dn2 = send(tblock(1, high), tblock(2, high), "t", "t", dy=DOWN)
     sy_up2 = send(S.at[3, *upper], S.at[2, *upper], dy=UP)
     sy_dn2 = send(S.at[1, *lower], S.at[2, *lower], dy=DOWN)
     a_up = send(S.at[0, *own_x], S.at[3, *own_x], dy=UP)
@@ -253,9 +259,9 @@
     v_dn.wait_recv()
     v_dn2 = send(wslab(UP, 1), wslab(UP, 1), "w", dz=DOWN)
     v_up.wait_recv()
-    w_sib.append(send(wslab(DOWN), wslab(DOWN), "w", dk=1))
+    w_sib.append(send(wslab(DOWN), wslab(DOWN), "w", "w", dk=1))
     w_dn.wait_recv()
-    w_sib.append(send(wslab(UP), wslab(UP), "w", dk=1))
+    w_sib.append(send(wslab(UP), wslab(UP), "w", "w", dk=1))
 
     sx.wait_recv()
     b_dn = send(S.at[0, *far_x], S.at[1, *far_x], dy=DOWN)
@@ -264,19 +270,19 @@
 
     w_up2.wait_recv()
     v_dn2.wait_recv()
-    w_sib.append(send(wslab(2), wslab(2), "w", dk=1))
+    w_sib.append(send(wslab(2), wslab(2), "w", "w", dk=1))
     p_x.wait_recv()
-    p_sib.append(send(pblock(1), pblock(1), dk=1))
+    p_sib.append(send(pblock(1), pblock(1), land="p", dk=1))
     q_dn = send(pblock(1), pblock(1), dz=DOWN)
     q_up = send(pblock(1), pblock(1), dz=UP)
     p_up.wait_recv()
     p_up2 = send(pblock(0, DOWN), pblock(0, DOWN), dz=UP)
-    p_sib.append(send(pblock(0, DOWN), pblock(0, DOWN), dk=1))
+    p_sib.append(send(pblock(0, DOWN), pblock(0, DOWN), land="p", dk=1))
     p_dn.wait_recv()
-    p_sib.append(send(pblock(0, UP), pblock(0, UP), dk=1))
-
-    for copy in t_up1, t_dn1, t_up2, t_dn2, *w_sib:
-        copy.wait_recv()
+    p_sib.append(send(pblock(0, UP), pblock(0, UP), land="p", dk=1))
+
+    await_group(landing["t"])
+    await_group(landing["w"])
 
     def product(rows, col0, n):
         cols = pl.ds(pl.multiple_of(col0 + 256 * n, 256), 256)
@@ -310,18 +316,18 @@
 
     q_dn.wait_recv()
     q_dn2 = send(pblock(1, UP), pblock(1, UP), dz=DOWN)
-    p_sib.append(send(pblock(1, UP), pblock(1, UP), dk=1))
+    p_sib.append(send(pblock(1, UP), pblock(1, UP), land="p", dk=1))
     q_up.wait_recv()
-    p_sib.append(send(pblock(1, DOWN), pblock(1, DOWN), dk=1))
+    p_sib.append(send(pblock(1, DOWN), pblock(1, DOWN), land="p", dk=1))
     p_up2.wait_recv()
-    p_sib.append(send(pblock(0, 2), pblock(0, 2), dk=1))
+    p_sib.append(send(pblock(0, 2), pblock(0, 2), land="p", dk=1))
     first, second, last = [pl.ds(*piece) for piece in PIECES]
     a_up.wait_recv()
     a_up2, a_up3 = [send(S.at[3, own, n], S.at[2, own, n], dy=UP) for n in (first, second)]
     b_dn.wait_recv()
     b_dn2, b_dn3 = [send(S.at[1, far, n], S.at[2, far, n], dy=DOWN) for n in (first, second)]
     q_dn2.wait_recv()
-    p_sib.append(send(pblock(1, 2), pblock(1, 2), dk=1))
+    p_sib.append(send(pblock(1, 2), pblock(1, 2), land="p", dk=1))
 
     def mapped(r):
         @pl.loop(0, 2)
@@ -371,8 +377,7 @@
             H[rows, :] = h * gains
             col[rows, :] = jnp.broadcast_to(jnp.sum(h * h, axis=1, keepdims=True), (16, 128))
 
-    for copy in p_sib:
-        copy.wait_recv()
+    await_group(landing["p"])
     sxy[0].wait_recv()
     mapped(0)
     sent("t")
@@ -422,6 +427,8 @@
     a_up3.wait_recv()
     b_dn3.wait_recv()
     mapped_part(second, True)
+    sxy[3].wait_recv()
+    mapped_part(y_cols, True)
     await_group(sq_c)
     total = sq[0]
     for i in range(1, 8):
@@ -442,10 +449,9 @@
             T[pl.ds(0, 256), pl.ds(768, 256)], E[pl.ds(768, 256), cols], preferred_element_type=F32
         )
 
-    sxy[3].wait_recv()
     a_up4.wait_recv()
     b_dn4.wait_recv()
-    mapped_part(pl.ds(PIECES[2][0], 4096 - PIECES[2][0]), True)
+    mapped_part(last, True)
     acc = errors(2, acc)
 
     tile = jnp.where(row == 0, jnp.max(amax_in), jnp.where(row == 1, jnp.max(amax_w), jnp.sum(acc)))
@@ -599,13 +605,7 @@
 
     for n in (UP, DOWN):
         b_1[0, n].wait_recv()
-        a_2[0, n].wait_recv()
-    b_2.wait_recv()
-    scale = 1.0 / math.sqrt(tokens_all)
-    for (first, count), landed in (
-        (b_rows, [(rb1, 0), (rb1, 1), (rb2, 0)]),
-        (a_rows, [(ra2, 0), (ra2, 1)]),
-    ):
+    for (first, count), landed in ((a_rows, []), (b_rows, [(rb1, 0), (rb1, 1)])):
 
         @pl.loop(0, count // 16)
         def _(i):
@@ -614,10 +614,13 @@
             total = W[3, mine, pl.ds(0, 1024)].astype(F32)
             for ref, index in landed:
                 total = total + ref[index, here, :].astype(F32)
-            total_g[pl.ds(pl.multiple_of(first + 16 * i, 16), 16), :] = total * scale
+            total_g[pl.ds(pl.multiple_of(first + 16 * i, 16), 16), :] = total
 
         rows = pl.ds(first, count)
         written.append(load(total_g.at[rows], parts.at[rows]))
+    for n in (UP, DOWN):
+        a_2[0, n].wait_recv()
+    b_2.wait_recv()
 
     assert len(groups) <= SEND_SEMS and len(received) <= RECV_SEMS
     for group in groups:
@@ -628,24 +631,28 @@
 
 
 def results(
-    tokens_all, parts, hist_in, hist_w, grad, loss, hist_in_new, hist_w_new,
-    held, tile, s_in, s_w, s_in_new, s_w_new, s_loss, sem_in, sem_out,
+    tokens_all, parts, ra2, rb2, hist_in, hist_w, grad, loss, hist_in_new, hist_w_new,
+    held, late_a, late_b, tile, s_in, s_w, s_in_new, s_w_new, s_loss, sem_in, sem_out,
 ):
-    pieces = [pl.ds(64 * i, 64) for i in range(4)]
+    a_rows, b_rows = pl.ds(0, AROWS), pl.ds(AROWS, 256 - AROWS)
     copies = [
         (parts.at[pl.ds(256, 8), pl.ds(0, 128)], tile),
         (hist_in, s_in),
         (hist_w, s_w),
-        *((parts.at[rows], held.at[rows]) for rows in pieces),
+        (parts.at[a_rows], held.at[a_rows]),
+        (ra2, late_a),
+        (parts.at[b_rows], held.at[b_rows]),
+        (rb2, late_b),
     ]
     copies = [pltpu.make_async_copy(a, b, sem_in.at[i]) for i, (a, b) in enumerate(copies)]
     for copy in copies:
         copy.start()
     backs = [
-        *((held.at[rows], grad.at[rows]) for rows in pieces),
         (s_in_new, hist_in_new),
         (s_w_new, hist_w_new),
         (s_loss, loss),
+        (held.at[a_rows], grad.at[a_rows]),
+        (held.at[b_rows], grad.at[b_rows]),
     ]
     backs = [pltpu.make_async_copy(a, b, sem_out.at[i]) for i, (a, b) in enumerate(backs)]
     for copy in copies[:3]:
@@ -656,11 +663,23 @@
     for i in range(15):
         s_in_new[i + 1] = s_in[i]
         s_w_new[i + 1] = s_w[i]
-    for back in backs[4:]:
+    for back in backs[:3]:
         back.start()
-    for copy, back in zip(copies[3:], backs):
-        copy.wait()
-        back.start()
+    scale = 1.0 / math.sqrt(tokens_all)
+    for first, count, late, n in (0, AROWS, late_a, 2), (AROWS, 256 - AROWS, late_b, 1):
+        for copy in copies[3:5] if first == 0 else copies[5:]:
+            copy.wait()
+
+        @pl.loop(0, count // 16)
+        def _(i):
+            here = pl.ds(pl.multiple_of(16 * i, 16), 16)
+            rows = pl.ds(pl.multiple_of(first + 16 * i, 16), 16)
+            total = held[rows, :]
+            for index in range(n):
+                total = total + late[index, here, :].astype(F32)
+            held[rows, :] = total * scale
+
+        backs[3 if first == 0 else 4].start()
     for back in backs:
         back.wait()
 
@@ -671,12 +690,16 @@
 ):
     tokens_all = teacher_in.shape[0] * lax.axis_size("context")
     hbm = pl.BlockSpec(memory_space=pl.ANY)
-    parts = pl.pallas_call(
+    parts, late_a, late_b = pl.pallas_call(
         functools.partial(kernel, tokens_all),
         name="distill",
-        out_shape=jax.ShapeDtypeStruct((264, 1024), F32),
+        out_shape=(
+            jax.ShapeDtypeStruct((264, 1024), F32),
+            jax.ShapeDtypeStruct((2, AROWS, 1024), BF16),
+            jax.ShapeDtypeStruct((1, 256 - AROWS, 1024), BF16),
+        ),
         in_specs=[hbm] * 9,
-        out_specs=hbm,
+        out_specs=(hbm,) * 3,
         scratch_shapes=[
             pltpu.VMEM((1024, 2048), BF16),
             pltpu.VMEM((4, 512, 2048), BF16),
@@ -695,9 +718,7 @@
             pltpu.VMEM((19, 8, 128), F32),
             pltpu.VMEM((8, 256, 1024), BF16),
             pltpu.VMEM((4, AROWS, 1024), BF16),
-            pltpu.VMEM((2, AROWS, 1024), BF16),
             pltpu.VMEM((4, 256 - AROWS, 1024), BF16),
-            pltpu.VMEM((1, 256 - AROWS, 1024), BF16),
             pltpu.VMEM((2, 64, 1024), BF16),
             pltpu.VMEM((4, 80, 1024), BF16),
             pltpu.VMEM((256, 1024), F32),
@@ -735,16 +756,18 @@
             jax.ShapeDtypeStruct((16,), F32),
             jax.ShapeDtypeStruct((16,), F32),
         ),
-        in_specs=[hbm] * 3,
+        in_specs=[hbm] * 5,
         out_specs=(hbm,) * 4,
         scratch_shapes=[
             pltpu.VMEM((256, 1024), F32),
+            pltpu.VMEM((2, AROWS, 1024), BF16),
+            pltpu.VMEM((1, 256 - AROWS, 1024), BF16),
             pltpu.VMEM((8, 128), F32),
             *(pltpu.SMEM((n,), F32) for n in (16, 16, 16, 16, 1)),
             pltpu.SemaphoreType.DMA((7,)),
-            pltpu.SemaphoreType.DMA((7,)),
+            pltpu.SemaphoreType.DMA((5,)),
         ],
-    )(parts, input_history, weight_history)
+    )(parts, late_a, late_b, input_history, weight_history)
     return grad, loss.reshape(()), hist_in, hist_w
 
 

time: 150 us -> 150 us (level)
  no operation moved by 1% of the time
where the time goes in v7:
time: 150 us; the launch traced here: 149 us
  Pallas kernels  149 us (99%)
    pallas_call x1, Pallas kernels, local(): pl.pallas_call(functools.partial(kernel, tokens_all), name='distill', out...  146 us

profile of v7, /device:TPU:0, one launch (start us, length us, event | category | flops | bytes accessed | tf_op | source)
XLA Modules:
  0.0 149.4 jit_solution(5700883286107800848)
XLA Ops:
  0.6 146.3 %distill.1 = (f32[264,1024]{1,0:T(8,128)}, bf16[2,112,1024]{2,1,0:T(8,128)(2,1)}, bf16[1,144,1024]{2,1,0:T(8,128)(2,1)}) custom-call(f32[16]{0:T(128)} %hist_in.1, f32[16]{0:T(128)} %hist_w.1, f32[1,4096]{1,0:T(1,128)} %bitcast.4, f32[1,8192]{1,0:T(1,128)} %bitcast.3, bf16[1024,512]{1,0:T(8,128)(2,1)} %tin.1, bf16[1024,1024]{1,0:T(8,128)(2,1)} %resid.1, ...), custom_call_target="tpu_custom_call" | custom-call | flops 25769803776 | bytes 16777216 | tf_op jit(solution)/shard_map/distill/pallas_call | solution.py:693
  146.9 2.4 %results.1 = (f32[256,1024]{1,0:T(8,128)}, f32[1]{0:T(128)}, f32[16]{0:T(128)}, f32[16]{0:T(128)}) custom-call(f32[264,1024]{1,0:T(8,128)} %get-tuple-element.11.parts, bf16[2,112,1024]{2,1,0:T(8,128)(2,1)} %get-tuple-element.12.ra2, bf16[1,144,1024]{2,1,0:T(8,128)(2,1)} %get-tuple-element.13.rb2, f32[16]{0:T(128)} %hist_in.1, f32[16]{0:T(128)} %hist_w.1), custom_call_target="tpu_custom_call" | custom-call | tf_op jit(solution)/shard_map/results/pallas_call | solution.py:750

commit v8 on v7

--- a/solution.py
+++ b/solution.py
@@ -360,7 +360,7 @@
             ref[pl.ds(row0 + 256 * own, 256), pl.ds(col0 + 256 * r, 256)] = S[r, :, cols].T
 
     def turn_first(r):
-        for g in range(4):
+        for g in range(6):
             turn(g, r)
 
     l_tgain.wait()
@@ -408,6 +408,10 @@
     a_up4 = send(S.at[3, own, last], S.at[2, own, last], dy=UP)
     b_dn4 = send(S.at[1, far, last], S.at[2, far, last], dy=DOWN)
     turn_first(1)
+    sent("r")
+    for r in (0, 3, 1):
+        turn(6, r)
+        turn(7, r)
 
     def errors(r, acc):
         for b in range(2):
@@ -467,11 +471,10 @@
     sc1 = send_all([(scal.at[t], scal.at[t], {"dy": dy, "dxl": dx}) for dy, dx in TENSOR], "s")
 
     sent("w")
-    sent("r")
 
     a_rows, b_rows = (0, AROWS), (AROWS, 256 - AROWS)
-    a_up_rows, a_dn_rows = (0, 48), (48, AROWS - 48)
-    b_up_rows, b_dn_rows = (AROWS, 80), (AROWS + 80, 176 - AROWS)
+    a_up_rows, a_dn_rows = (0, 80), (80, AROWS - 80)
+    b_up_rows, b_dn_rows = (AROWS, 64), (AROWS + 64, 192 - AROWS)
 
     def gslot(dxh, dz, rows=(0, 256), other=0):
         g = ORDER.index((dxh, dz))
@@ -487,17 +490,22 @@
         def _(n):
             at = pl.multiple_of(512 * n, 512)
             rows, cols = pl.ds(row0 + 256 * own, 256), pl.ds(at, 512)
-            if (g, own) == (0, 0):
-                one = M[rows, cols] + jnp.dot(
-                    ref[rows, pl.ds(512, 256)], E[pl.ds(512, 256), cols], preferred_element_type=F32
-                )
-            else:
-                one = jnp.dot(ref[rows, pl.ds(col0, 1024)], E[:, cols], preferred_element_type=F32)
+            one = jnp.dot(ref[rows, pl.ds(col0, 1024)], E[:, cols], preferred_element_type=F32)
             start = pl.multiple_of(1024 * (1 - own) + at, 512)
             W[g // 2, pl.ds(256 * (g % 2), 256), pl.ds(start, 512)] = one.astype(BF16)
 
         if own == 0:
             to_sib.append(send(gslot(dxh, dz, other=1), sib.at[g], dk=1))
+
+    def first_half_term():
+        for n in range(2):
+            cols, there = pl.ds(512 * n, 512), pl.ds(1024 + 512 * n, 512)
+            one = M[pl.ds(0, 256), cols] + jnp.dot(
+                T[pl.ds(0, 256), pl.ds(512, 256)], E[pl.ds(512, 256), cols], preferred_element_type=F32
+            )
+            W[0, pl.ds(0, 256), there] = one.astype(BF16)
+            send(W.at[0, pl.ds(0, 256), there], sib.at[0, pl.ds(0, 256), cols], land="first", dk=1)
+        to_sib.append(None)
 
     def term(g):
         dxh, dz = ORDER[g]
@@ -517,12 +525,12 @@
 
         to_sib.append(send(gslot(dxh, dz, other=1), sib.at[g], dk=1))
 
-    def add(dxh, dz, rows, others):
+    def add(dxh, dz, rows, others, base=0):
         g = ORDER.index((dxh, dz))
 
         @pl.loop(0, rows[1] // 16)
         def _(i):
-            here = pl.ds(pl.multiple_of(16 * i, 16), 16)
+            here = pl.ds(pl.multiple_of(base + 16 * i, 16), 16)
             there = pl.ds(pl.multiple_of(256 * (g % 2) + rows[0] + 16 * i, 16), 16)
             total = W[g // 2, there, pl.ds(0, 1024)].astype(F32)
             for ref, index in others:
@@ -554,17 +562,19 @@
         along_z(0, dz, a_rows, a_up_rows, a_dn_rows, am, 0, ra2, a_2, a_m)
 
     def term_of(g):
-        for r in range(4) if g >= 4 else (2,):
-            turn(g, r)
+        turn(g, 2)
         term(g)
 
     turn(0, 2)
-    half_term(0, 0)
+    first_half_term()
     half_term(0, 1)
     turn(1, 2)
     half_term(1, 0)
-    finish(0)
+    await_group(landing["first"])
+    add(1, 2, b_rows, [(sib, 0)], AROWS)
     second_b(1, 2)
+    add(1, 2, a_rows, [(sib, 0)])
+    a_1[2] = send(gslot(1, 2, a_rows), ra1.at[2], dxh=1)
     half_term(1, 1)
     await_group(sc1)
     at = 8 + xh * 4 + z
@@ -719,8 +729,8 @@
             pltpu.VMEM((8, 256, 1024), BF16),
             pltpu.VMEM((4, AROWS, 1024), BF16),
             pltpu.VMEM((4, 256 - AROWS, 1024), BF16),
-            pltpu.VMEM((2, 64, 1024), BF16),
-            pltpu.VMEM((4, 80, 1024), BF16),
+            pltpu.VMEM((2, 96, 1024), BF16),
+            pltpu.VMEM((4, 96, 1024), BF16),
             pltpu.VMEM((256, 1024), F32),
             pltpu.VMEM((1, 4096), F32),
             pltpu.VMEM((1, 1024), F32),

time: 150 us -> 149 us (level)
  no operation moved by 1% of the time
where the time goes in v8:
time: 149 us
  Pallas kernels  148 us (99%)
    pallas_call x1, Pallas kernels, local(): pl.pallas_call(functools.partial(kernel, tokens_all), name='distill', out...  146 us

profile of v8, /device:TPU:0, one launch (start us, length us, event | category | flops | bytes accessed | tf_op | source)
XLA Modules:
  0.0 148.6 jit_solution(6187164820749865638)
XLA Ops:
  0.6 145.5 %distill.1 = (f32[264,1024]{1,0:T(8,128)}, bf16[2,112,1024]{2,1,0:T(8,128)(2,1)}, bf16[1,144,1024]{2,1,0:T(8,128)(2,1)}) custom-call(f32[16]{0:T(128)} %hist_in.1, f32[16]{0:T(128)} %hist_w.1, f32[1,4096]{1,0:T(1,128)} %bitcast.4, f32[1,8192]{1,0:T(1,128)} %bitcast.3, bf16[1024,512]{1,0:T(8,128)(2,1)} %tin.1, bf16[1024,1024]{1,0:T(8,128)(2,1)} %resid.1, ...), custom_call_target="tpu_custom_call" | custom-call | flops 25769803776 | bytes 16777216 | tf_op jit(solution)/shard_map/distill/pallas_call | solution.py:703
  146.2 2.4 %results.1 = (f32[256,1024]{1,0:T(8,128)}, f32[1]{0:T(128)}, f32[16]{0:T(128)}, f32[16]{0:T(128)}) custom-call(f32[264,1024]{1,0:T(8,128)} %get-tuple-element.11.parts, bf16[2,112,1024]{2,1,0:T(8,128)(2,1)} %get-tuple-element.12.ra2, bf16[1,144,1024]{2,1,0:T(8,128)(2,1)} %get-tuple-element.13.rb2, f32[16]{0:T(128)} %hist_in.1, f32[16]{0:T(128)} %hist_w.1), custom_call_target="tpu_custom_call" | custom-call | tf_op jit(solution)/shard_map/results/pallas_call | solution.py:760

commit v9 on v8

--- a/solution.py
+++ b/solution.py
@@ -298,7 +298,7 @@
             cols = pl.ds(pl.multiple_of(256 * n, 256), 256)
             psend[rows, cols] = product(rows, 1024 * (1 - xl), n).astype(BF16)
 
-        for rows in (rows,) if q < 3 else (pl.ds(768, 128), pl.ds(896, 128)):
+        for rows in (rows,) if q < 3 else (pl.ds(768, 192), pl.ds(960, 64)):
             rs_t.append(send(psend.at[rows], precv.at[rows], "r", dxl=1))
 
 
@@ -368,7 +368,7 @@
 
     def squares(q):
         rs_t[q].wait_recv()
-        first, count = (256 * q, 256) if q < 3 else (128 * q + 384, 128)
+        first, count = (256 * q, 256) if q < 3 else (192 * q + 192, 192 if q == 3 else 64)
 
         @pl.loop(0, count // 16)
         def _(i):

time: 149 us -> 150 us (level)
  no operation moved by 1% of the time
where the time goes in v9:
time: 150 us; the launch traced here: 149 us
  Pallas kernels  148 us (99%)
    pallas_call x1, Pallas kernels, local(): pl.pallas_call(functools.partial(kernel, tokens_all), name='distill', out...  146 us

profile of v9, /device:TPU:0, one launch (start us, length us, event | category | flops | bytes accessed | tf_op | source)
XLA Modules:
  0.0 149.0 jit_solution(10130654302838356756)
XLA Ops:
  0.6 145.9 %distill.1 = (f32[264,1024]{1,0:T(8,128)}, bf16[2,112,1024]{2,1,0:T(8,128)(2,1)}, bf16[1,144,1024]{2,1,0:T(8,128)(2,1)}) custom-call(f32[16]{0:T(128)} %hist_in.1, f32[16]{0:T(128)} %hist_w.1, f32[1,4096]{1,0:T(1,128)} %bitcast.4, f32[1,8192]{1,0:T(1,128)} %bitcast.3, bf16[1024,512]{1,0:T(8,128)(2,1)} %tin.1, bf16[1024,1024]{1,0:T(8,128)(2,1)} %resid.1, ...), custom_call_target="tpu_custom_call" | custom-call | flops 25769803776 | bytes 16777216 | tf_op jit(solution)/shard_map/distill/pallas_call | solution.py:703
  146.6 2.4 %results.1 = (f32[256,1024]{1,0:T(8,128)}, f32[1]{0:T(128)}, f32[16]{0:T(128)}, f32[16]{0:T(128)}) custom-call(f32[264,1024]{1,0:T(8,128)} %get-tuple-element.11.parts, bf16[2,112,1024]{2,1,0:T(8,128)(2,1)} %get-tuple-element.12.ra2, bf16[1,144,1024]{2,1,0:T(8,128)(2,1)} %get-tuple-element.13.rb2, f32[16]{0:T(128)} %hist_in.1, f32[16]{0:T(128)} %hist_w.1), custom_call_target="tpu_custom_call" | custom-call | tf_op jit(solution)/shard_map/results/pallas_call | solution.py:760
